TPU v7x, 128 devices: a whole 4x4x4 slice. The times are simulated.
128 devices in a mesh: dom: 32 (over z, x, core), sub: 4 (over y).
Axes of the slice: x: 4, y: 4, z: 4, core: 2. Of those that a mesh axis runs over, the one named last changes fastest.
Arguments:
- leaf_mult: bfloat16 [131072, 488], P(('dom', 'sub')), may hold values from -6 to 6
- m2m: bfloat16 [8, 488, 488], replicated, may hold values from -0.09375 to 0.09375
- compress: bfloat16 [488, 128], replicated, may hold values from -0.25 to 0.25
- m2l_core: bfloat16 [316, 128, 128], P('sub'), may hold values from -0.0390625 to 0.0390625
- expand: bfloat16 [128, 488], replicated, may hold values from -0.5 to 0.5
- l2l: bfloat16 [488, 8, 488], replicated, may hold values from -0.25 to 0.25
- inherited: bfloat16 [131072, 488], P(('dom', 'sub')), may hold values from -6 to 6
- send_rows: int32 [32, 32, 32], P('dom'), may hold values from 0 to 511, as said below
- m2l_list: int32 [16384, 316], P('dom', 'sub'), may hold values from -1 to 1535, as said below
Outputs:
- leaf_local: bfloat16 [131072, 488], P(('dom', 'sub'))
Inputs may be any that keep to these rules, and one draw needn't show every extreme that they name: Rows of the sending partition; send_rows[0, 1, 0] is 511 and send_rows[0, 1, 1] is 0. A program may pack several of these whole-number row indices into one word while they travel. `m2l_list`: A target of partition p refers to a received slot j from partition s (s != p) only if j < min(32, max(16, 32 >> (|s - p| - 1))); slots of s = p are never referred to.
All inputs are finite; a program needn't handle non-finite values.
Results may differ from a plain program's by a relative error of at most 0.017.
Values may be sent and summed in bfloat16 or wider, within the bound.
No kernel may reach another device: no remote copies, remote signals or barrier semaphores. Data moves between devices by JAX's collectives and lax.ppermute only.
A program may use at most 64 MiB of HBM per device.

v0:
```python
import math

import jax
import jax.numpy as jnp
from jax import lax
from jax.sharding import PartitionSpec as P


def local(leaf_mult, m2m, compress, m2l_core, expand, l2l, inherited, send_rows, m2l_list):
    width = leaf_mult.shape[1]
    nkids = m2m.shape[0]
    rank_width = compress.shape[1]
    parents = jnp.dot(
        leaf_mult.reshape(-1, nkids * width),
        m2m.reshape(nkids * width, width),
        preferred_element_type=jnp.float32,
    ).astype(jnp.bfloat16)
    packed = jnp.dot(parents, compress, preferred_element_type=jnp.float32).astype(jnp.bfloat16)
    part_rows = lax.all_gather(packed, "sub", axis=0, tiled=True)
    npart = lax.axis_size("dom")
    oct_part = part_rows.shape[0]
    everything = lax.all_gather(part_rows, "dom", axis=0, tiled=True)
    lists = lax.all_gather(send_rows, "dom", axis=0, tiled=True)
    wanted = jnp.take(lists, lax.axis_index("dom"), axis=1)
    global_rows = (jnp.arange(npart, dtype=jnp.int32)[:, None] * oct_part + wanted).reshape(-1)
    arrived = jnp.take(everything, global_rows, axis=0)
    table = jnp.concatenate([part_rows, arrived], axis=0)
    table_rows = table.shape[0]
    positions = jnp.arange(table_rows, dtype=jnp.int32)
    offsets = m2l_core.shape[0]
    core_flat = m2l_core.reshape(offsets * rank_width, rank_width)
    count = lax.axis_size("sub") * parents.shape[0]
    block = math.gcd(count, 64)
    listed = m2l_list.reshape(count // block, block, offsets)

    def one_block(entries):
        onehot = (entries[:, :, None] == positions).astype(jnp.bfloat16)
        picked = jnp.einsum(
            "tkr,rd->tkd", onehot, table, preferred_element_type=jnp.float32
        ).astype(jnp.bfloat16)
        return jnp.dot(
            picked.reshape(block, offsets * rank_width),
            core_flat,
            preferred_element_type=jnp.float32,
        )

    acc = lax.psum_scatter(
        lax.map(one_block, listed).reshape(count, rank_width).astype(jnp.bfloat16),
        "sub",
        scatter_dimension=0,
        tiled=True,
    )
    parent_local = jnp.dot(acc, expand, preferred_element_type=jnp.float32).astype(jnp.bfloat16)
    children = jnp.dot(
        parent_local, l2l.reshape(width, nkids * width), preferred_element_type=jnp.float32
    )
    result = children.reshape(-1, width) + inherited.astype(jnp.float32)
    return result.astype(jnp.bfloat16)


def solution(mesh):
    placed = (
        P(("dom", "sub"), None),
        P(),
        P(),
        P("sub", None, None),
        P(),
        P(),
        P(("dom", "sub"), None),
        P("dom", None, None),
        P("dom", "sub"),
    )
    return jax.shard_map(
        local, mesh=mesh, in_specs=placed, out_specs=P(("dom", "sub"), None), check_vma=False
    )
```

profile of v0, /device:TPU:1, one launch (start us, length us, event | category | flops | bytes accessed | tf_op | source)
XLA Modules:
  0.0 184.6 jit_solution(14801734909629032412)
XLA Ops:
  6.5 0.0 copy-start
  6.5 0.0 all-gather.2.cloned.1.call-start
  6.5 1.5 copy.22
  8.1 1.8 reshape.81
  9.9 0.0 copy-done.4
  9.9 0.0 copy-start.5
  9.9 0.0 copy-start.3
  9.9 4.1 %fusion.17 = bf16[128,128]{1,0:T(8,128)(2,1)S(1)} fusion(bf16[488,128]{1,0:T(8,128)(2,1)S(1)} %copy-done.4, bf16[128,3904]{1,0:T(8,128)(2,1)S(1)} %reshape.81, bf16[3904,488]{1,0:T(8,128)(2,1)} %bitcast.44), kind=kOutput, calls=%fused_computation.18 | convolution fusion | flops 503788544 | bytes 4967424 | tf_op jit(solution)/shard_map/dot_general | solution.py:18
  14.0 0.0 copy-start.1
  14.0 11.3 %all_gather.9 = bf16[512,128]{1,0:T(8,128)(2,1)} all-gather(bf16[128,128]{1,0:T(8,128)(2,1)S(1)} %fusion.17), channel_id=1, replica_groups=mesh['dom'=32,'sub'=4] {'sub'}, dimensions={0}, use_global_device_ids=true | all-gather | bytes 163840 | tf_op jit(solution)/shard_map/all_gather | solution.py:19
  25.3 0.0 all-gather.2.cloned.1.call-update
  25.4 0.0 reduce-scatter.2.cloned.1.call-start
  25.4 0.0 copy-done.5
  25.5 29.8 %all_gather.10 = s32[32,32,32]{2,1,0:T(8,128)S(1)} all-gather(s32[1,32,32]{2,1,0:T(8,128)S(1)} %copy-done.5), channel_id=1, replica_groups=mesh['dom'=32,'sub'=4] {'dom'}, dimensions={0}, use_global_device_ids=true | all-gather | bytes 135168 | tf_op jit(solution)/shard_map/all_gather | solution.py:23
  55.3 0.1 broadcast_add_fusion
  55.4 0.1 add.63
  55.4 0.1 add.60
  55.5 0.0 copy-done.3
  55.5 0.1 copy.21
  55.7 21.4 %all-gather.2.cloned.1.call-done = bf16[16384,128]{1,0:T(8,128)(2,1)} async-done(((bf16[512,128]{1,0:T(8,128)(2,1)}), bf16[16384,128]{1,0:T(8,128)(2,1)}) %all-gather.2.cloned.1.call-update) | async-done | bytes 4194320 | tf_op jit(solution)/shard_map/all_gather | solution.py:22
  77.1 5.6 %gather_fusion = bf16[1024,128]{1,0:T(8,128)(2,1)S(1)} fusion(bf16[16384,128]{1,0:T(8,128)(2,1)} %all-gather.2.cloned.1.call-done, s32[1024]{0:T(1024)S(1)} %broadcast_clamp_fusion), kind=kCustom, calls=%fused_computation | custom fusion | bytes 528384 | tf_op jit(solution)/shard_map/jit(_take)/gather | solution.py:26
  82.7 0.2 broadcast_select_fusion
  82.9 0.0 copy-done.2
  82.9 0.8 pad_maximum_fusion
  83.7 64.1 %while.12 = (s32[]{:T(128)}, bf16[8,64,128]{2,1,0:T(8,128)(2,1)}, s32[8,64,79]{2,1,0:T(8,128)S(1)}, bf16[1536,128]{1,0:T(8,128)(2,1)}, bf16[10112,128]{1,0:T(8,128)(2,1)S(1)}, /*index=5*/s32[]{:T(128)}) while((s32[]{:T(128)}, bf16[8,64,128]{2,1,0:T(8,128)(2,1)}, s32[8,64,79]{2,1,0:T(8,128)S(1)}, bf16[1536,128]{1,0:T(8,128)(2,1)}, ...), condition=%wide.region_1.2_spmd.clone, body=%wide.region_0.1_spmd.clone.sunk | while | flops 2162188288 | bytes 5664085 | solution.py:48
  83.7 6.8 %fusion.33 = bf16[64,79,128]{2,1,0:T(8,128)(2,1)S(1)} fusion(s32[64,79]{1,0:T(8,128)S(1)} %dynamic-slice_bitcast_fusion.2, bf16[1536,128]{1,0:T(8,128)(2,1)} %get-tuple-element.117), kind=kOutput, calls=%fused_computation.5.clone.1 | convolution fusion | flops 1996513280 | bytes 1707776 | tf_op jit(solution)/shard_map/while/body/eval_jaxpr/tkr,rd->tkd/dot_general | solution.py:38
  90.4 1.2 fusion.34
  91.7 6.8 %fusion.33 = bf16[64,79,128]{2,1,0:T(8,128)(2,1)S(1)} fusion(s32[64,79]{1,0:T(8,128)S(1)} %dynamic-slice_bitcast_fusion.2, bf16[1536,128]{1,0:T(8,128)(2,1)} %get-tuple-element.117), kind=kOutput, calls=%fused_computation.5.clone.1 | convolution fusion | flops 1996513280 | bytes 1707776 | tf_op jit(solution)/shard_map/while/body/eval_jaxpr/tkr,rd->tkd/dot_general | solution.py:38
  98.5 1.2 fusion.34
  99.7 6.8 %fusion.33 = bf16[64,79,128]{2,1,0:T(8,128)(2,1)S(1)} fusion(s32[64,79]{1,0:T(8,128)S(1)} %dynamic-slice_bitcast_fusion.2, bf16[1536,128]{1,0:T(8,128)(2,1)} %get-tuple-element.117), kind=kOutput, calls=%fused_computation.5.clone.1 | convolution fusion | flops 1996513280 | bytes 1707776 | tf_op jit(solution)/shard_map/while/body/eval_jaxpr/tkr,rd->tkd/dot_general | solution.py:38
  106.5 1.2 fusion.34
  107.7 6.8 %fusion.33 = bf16[64,79,128]{2,1,0:T(8,128)(2,1)S(1)} fusion(s32[64,79]{1,0:T(8,128)S(1)} %dynamic-slice_bitcast_fusion.2, bf16[1536,128]{1,0:T(8,128)(2,1)} %get-tuple-element.117), kind=kOutput, calls=%fused_computation.5.clone.1 | convolution fusion | flops 1996513280 | bytes 1707776 | tf_op jit(solution)/shard_map/while/body/eval_jaxpr/tkr,rd->tkd/dot_general | solution.py:38
  114.5 1.2 fusion.34
  115.7 6.8 %fusion.33 = bf16[64,79,128]{2,1,0:T(8,128)(2,1)S(1)} fusion(s32[64,79]{1,0:T(8,128)S(1)} %dynamic-slice_bitcast_fusion.2, bf16[1536,128]{1,0:T(8,128)(2,1)} %get-tuple-element.117), kind=kOutput, calls=%fused_computation.5.clone.1 | convolution fusion | flops 1996513280 | bytes 1707776 | tf_op jit(solution)/shard_map/while/body/eval_jaxpr/tkr,rd->tkd/dot_general | solution.py:38
  122.5 1.2 fusion.34
  123.7 6.8 %fusion.33 = bf16[64,79,128]{2,1,0:T(8,128)(2,1)S(1)} fusion(s32[64,79]{1,0:T(8,128)S(1)} %dynamic-slice_bitcast_fusion.2, bf16[1536,128]{1,0:T(8,128)(2,1)} %get-tuple-element.117), kind=kOutput, calls=%fused_computation.5.clone.1 | convolution fusion | flops 1996513280 | bytes 1707776 | tf_op jit(solution)/shard_map/while/body/eval_jaxpr/tkr,rd->tkd/dot_general | solution.py:38
  130.5 1.2 fusion.34
  131.7 6.8 %fusion.33 = bf16[64,79,128]{2,1,0:T(8,128)(2,1)S(1)} fusion(s32[64,79]{1,0:T(8,128)S(1)} %dynamic-slice_bitcast_fusion.2, bf16[1536,128]{1,0:T(8,128)(2,1)} %get-tuple-element.117), kind=kOutput, calls=%fused_computation.5.clone.1 | convolution fusion | flops 1996513280 | bytes 1707776 | tf_op jit(solution)/shard_map/while/body/eval_jaxpr/tkr,rd->tkd/dot_general | solution.py:38
  138.5 1.2 fusion.34
  139.7 6.8 %fusion.33 = bf16[64,79,128]{2,1,0:T(8,128)(2,1)S(1)} fusion(s32[64,79]{1,0:T(8,128)S(1)} %dynamic-slice_bitcast_fusion.2, bf16[1536,128]{1,0:T(8,128)(2,1)} %get-tuple-element.117), kind=kOutput, calls=%fused_computation.5.clone.1 | convolution fusion | flops 1996513280 | bytes 1707776 | tf_op jit(solution)/shard_map/while/body/eval_jaxpr/tkr,rd->tkd/dot_general | solution.py:38
  146.5 1.2 fusion.34
  147.7 0.0 reduce-scatter.2.cloned.1.call-update
  147.8 8.7 %reshape.84 = bf16[488,3904]{1,0:T(8,128)(2,1)} reshape(bf16[488,8,488]{2,1,0:T(8,128)(2,1)} %param.16) | data formatting | bytes 7620608 | tf_op jit(solution)/shard_map/reshape | solution.py:55
  156.5 8.5 %reduce-scatter.2.cloned.1.call-done = bf16[128,128]{1,0:T(8,128)(2,1)} async-done(((bf16[512,128]{1,0:T(8,128)(2,1)}), bf16[128,128]{1,0:T(8,128)(2,1)}) %reduce-scatter.2.cloned.1.call-update) | async-done | bytes 32784 | tf_op jit(solution)/shard_map/reduce_scatter | solution.py:47
  165.0 4.5 %fusion.15 = f32[128,3904]{1,0:T(8,128)} fusion(bf16[488,3904]{1,0:T(8,128)(2,1)} %reshape.84, bf16[128,128]{1,0:T(8,128)(2,1)} %reduce-scatter.2.cloned.1.call-done, bf16[128,488]{0,1:T(8,128)(2,1)S(1)} %copy-done), kind=kOutput, calls=%fused_computation.16 | convolution fusion | flops 503772160 | bytes 5966848 | tf_op jit(solution)/shard_map/dot_general | solution.py:54
  169.5 3.4 %reshape.85 = f32[1024,488]{1,0:T(8,128)S(1)} reshape(f32[128,3904]{1,0:T(8,128)} %fusion.15) | data formatting | bytes 3997696 | tf_op jit(solution)/shard_map/reshape | solution.py:57
  172.8 1.8 copy.24
  174.7 3.1 %add_convert_fusion = bf16[1024,488]{0,1:T(8,128)(2,1)} fusion(f32[1024,488]{0,1:T(8,128)} %copy.24, bf16[1024,488]{0,1:T(8,128)(2,1)} %param.17), kind=kLoop, calls=%fused_computation.13 | loop fusion | flops 1499136 | bytes 3997696 | tf_op jit(solution)/shard_map/convert_element_type | solution.py:58
  (18 shorter events, 0.1 us)
Async XLA Ops:
  6.5 158.5 %copy-start = (bf16[128,488]{0,1:T(8,128)(2,1)S(1)}, bf16[128,488]{0,1:T(8,128)(2,1)}, u32[]{:S(2)}) copy-start(bf16[128,488]{0,1:T(8,128)(2,1)} %param.15) | copy-start | bytes 374788
  6.5 3.4 %copy-start.4 = (bf16[488,128]{1,0:T(8,128)(2,1)S(1)}, bf16[488,128]{1,0:T(8,128)(2,1)}, u32[]{:S(2)}) copy-start(bf16[488,128]{1,0:T(8,128)(2,1)} %param.13) | copy-start | bytes 374788
  6.5 70.5 %all-gather.2.cloned.1.call-start = ((), (), s32[]{:S(2)}) async-start(), calls=%async_computation.1 | async-start | bytes 4325376 | tf_op jit(solution)/shard_map/all_gather | solution.py:22
  9.9 15.5 %copy-start.5 = (s32[1,32,32]{2,1,0:T(8,128)S(1)}, s32[1,32,32]{2,1,0:T(8,128)}, u32[]{:S(2)}) copy-start(s32[1,32,32]{2,1,0:T(8,128)} %param.18) | copy-start | bytes 12292
  9.9 45.6 %copy-start.3 = (s32[512,79]{0,1:T(8,128)S(1)}, s32[512,79]{0,1:T(8,128)}, u32[]{:S(2)}) copy-start(s32[512,79]{0,1:T(8,128)} %param.19) | copy-start | bytes 485380
  14.0 69.7 %copy-start.1 = (bf16[79,128,128]{2,1,0:T(8,128)(2,1)S(1)}, bf16[79,128,128]{2,1,0:T(8,128)(2,1)}, u32[]{:S(2)}) copy-start(bf16[79,128,128]{2,1,0:T(8,128)(2,1)} %param.14) | copy-start | bytes 7766020
  25.3 57.5 %copy-start.2 = (bf16[512,128]{1,0:T(8,128)(2,1)S(1)}, bf16[512,128]{1,0:T(8,128)(2,1)}, u32[]{:S(2)}) copy-start(bf16[512,128]{1,0:T(8,128)(2,1)} %all_gather.9) | copy-start | bytes 393220
  25.4 139.6 %reduce-scatter.2.cloned.1.call-start = ((), (), s32[]{:S(2)}) async-start(), calls=%async_computation.2 | async-start | bytes 163840 | tf_op jit(solution)/shard_map/reduce_scatter | solution.py:47
Sparse Core Ops, SparseCore 0:
  25.5 51.5 all-gather.1
  147.9 17.0 reduce-scatter.1
where the time goes:
time: 187 us; the launch traced here: 185 us
  matrix products  72.5 us (39%)
  blocking collectives  41.1 us (22%)
  waiting for transfers between devices  29.9 us (16%)
  local copies, waits for them, and re-layouts  23.2 us (12%)
  between operations  13.6 us (7%)
  other arithmetic  4.18 us (2%)
    dot_general x8, matrix products, one_block(): jnp.einsum('tkr,rd->tkd', onehot, table, preferred_element_type=jnp.float32)  54.1 us
    all_gather x1, blocking collectives, local(): lists = lax.all_gather(send_rows, 'dom', axis=0, tiled=True)  29.8 us
    all_gather x1, waiting for transfers between devices, local(): everything = lax.all_gather(part_rows, 'dom', axis=0, tiled=True)  21.4 us
    all_gather x1, blocking collectives, local(): part_rows = lax.all_gather(packed, 'sub', axis=0, tiled=True)  11.3 us
    dot_general x8, matrix products, one_block(): jnp.dot(picked.reshape(block, offsets * rank_width), core_flat, preferred...  9.85 us
    reshape x1, local copies, waits for them, and re-layouts, local(): l2l.reshape(width, nkids * width)  8.73 us
    reduce_scatter x1, waiting for transfers between devices, local(): lax.psum_scatter(lax.map(one_block, listed).reshape(count, rank_width).as...  8.49 us
    gather x1, local copies, waits for them, and re-layouts, local(): arrived = jnp.take(everything, global_rows, axis=0)  5.61 us
  transfers between devices with their start and end apart: 2, of which 2 were waited for; matrix products, arithmetic and copies ran while one was open for 5% of the time, Pallas kernels for 0%

commit v1 on v0

v1 whole, which is shorter than its diff:
```python
import jax
import jax.numpy as jnp
from jax import lax
from jax.experimental import pallas as pl
from jax.experimental.pallas import tpu as pltpu
from jax.sharding import PartitionSpec as P

BF = jnp.bfloat16
F32 = jnp.float32
I32 = jnp.int32
MIB = 1 << 20
CAP = 32
SURE = 16
NONE = 1023

VMEM = pl.BlockSpec(memory_space=pltpu.VMEM)
ANY = pl.BlockSpec(memory_space=pl.ANY)


def dot(a, b):
    return jnp.dot(a, b, preferred_element_type=F32)


def call(kernel, name, out, ins, scratch, limit, flops, nbytes):
    return pl.pallas_call(
        kernel,
        name=name,
        out_shape=out,
        in_specs=ins,
        out_specs=jax.tree.map(lambda _: VMEM, out),
        scratch_shapes=scratch,
        compiler_params=pltpu.CompilerParams(vmem_limit_bytes=limit * MIB),
        cost_estimate=pl.CostEstimate(flops=flops, bytes_accessed=nbytes, transcendentals=0),
    )


def strided(ref, first, count, stride, width):
    parts = [ref[i, pl.ds(first, count, stride=stride), :] for i in range(ref.shape[0])]
    return jnp.concatenate(parts, axis=1)[:, :width].astype(BF)


def up_kernel(leaf_ref, m2m_ref, compress_ref, out_ref, rows_ref, m2m_buf, sems):
    nkids, width = m2m_ref.shape[0], m2m_ref.shape[1]
    count = leaf_ref.shape[1] // nkids
    copies = [
        pltpu.make_async_copy(m2m_ref.at[c], m2m_buf.at[c], sems.at[c]) for c in range(nkids)
    ]
    for copy in copies:
        copy.start()
    for j in range(leaf_ref.shape[1] // 128):
        cols = slice(j * 128, (j + 1) * 128)
        for i, base in enumerate(range(0, width, 128)):
            size = min(128, width - base)
            rows_ref[i, cols, :size] = leaf_ref[base:base + size, cols].astype(F32).T
    total = jnp.zeros((count, width), F32)
    for c in range(nkids):
        kid = strided(rows_ref, c, count, nkids, width)
        copies[c].wait()
        total = total + dot(kid, m2m_buf[c])
    out_ref[...] = dot(total.astype(BF), compress_ref[...]).astype(BF)


def upward(leaf_t, m2m, compress):
    nkids, width, _ = m2m.shape
    count = leaf_t.shape[1] // nkids
    return call(
        up_kernel,
        "upward",
        jax.ShapeDtypeStruct((count, compress.shape[1]), BF),
        [VMEM, ANY, VMEM],
        [
            pltpu.VMEM((-(-width // 128), leaf_t.shape[1], 128), F32),
            pltpu.VMEM(m2m.shape, BF),
            pltpu.SemaphoreType.DMA((nkids,)),
        ],
        24,
        2 * leaf_t.size * width,
        2 * (leaf_t.size + m2m.size),
    )(leaf_t, m2m, compress)


def pick_kernel(own_ref, one_ref, two_ref, three_ref, rows_ref, part_ref, send_ref):
    me = lax.axis_index("sub")
    count = own_ref.shape[0]
    for shift, ref in enumerate((own_ref, one_ref, two_ref, three_ref)):
        start = lax.rem(me + (4 - shift), 4) * count
        part_ref[pl.ds(pl.multiple_of(start, count), count), :] = ref[...]
    part = part_ref[...]
    wanted = rows_ref.shape[0]
    rows = jnp.broadcast_to(rows_ref[...], (wanted, 128)).astype(jnp.int16)
    lane = lax.broadcasted_iota(I32, (1, 128), 1)
    hot = jnp.concatenate(
        [
            jnp.where(rows == (lane + base).astype(jnp.int16), BF(1), BF(0))
            for base in range(0, part.shape[0], 128)
        ],
        axis=1,
    )
    send_ref[...] = dot(hot, part).astype(BF).reshape(send_ref.shape)


def pick(pieces, rows, npart):
    count, rank = pieces[0].shape
    return call(
        pick_kernel,
        "pick",
        (
            jax.ShapeDtypeStruct((4 * count, rank), BF),
            jax.ShapeDtypeStruct((npart, CAP, rank), BF),
        ),
        [VMEM] * 5,
        [],
        16,
        2 * rows.shape[0] * 4 * count * rank,
        2 * rows.shape[0] * rank,
    )(*pieces, rows)


def prep_kernel(list_ref, code_ref, extra_ref):
    part = lax.axis_index("dom")
    offsets, count = list_ref.shape
    value = list_ref[...]
    remote = value - count
    source = lax.shift_right_arithmetic(remote, 5)
    slot = remote & (CAP - 1)
    sure = slot < SURE
    below = source < part
    row = jnp.where(sure, source * SURE + slot, part * SURE + slot - SURE)
    far = jnp.where(sure | below, row + 1024, NONE)
    code = jnp.where(value < 0, NONE, jnp.where(value < count, value, far))
    extra = jnp.where((value >= count) & (slot >= SURE) & (source > part), slot - SURE, -1)
    pad = jnp.full((128 - offsets, count), -1, I32)
    code = jnp.concatenate([code, pad], axis=0)
    extra = jnp.concatenate([extra, pad], axis=0)
    for j in range(count // 128):
        cols = slice(j * 128, (j + 1) * 128)
        code_ref[cols, :] = code[:, cols].T
        extra_ref[cols, :] = extra[:, cols].astype(F32).T.astype(BF)


def prepare(list_t):
    offsets, count = list_t.shape
    return call(
        prep_kernel,
        "prepare",
        (jax.ShapeDtypeStruct((count, 128), I32), jax.ShapeDtypeStruct((count, 128), BF)),
        [VMEM],
        [],
        16,
        1,
        4 * list_t.size,
    )(list_t)


def split_kernel(l2l_ref, out_ref, wide_ref):
    width, nkids, _ = l2l_ref.shape
    for i, base in enumerate(range(0, width, 128)):
        size = min(128, width - base)
        block = l2l_ref[:, :, base:base + size].astype(F32)
        wide_ref[i, :, :size] = block.reshape(width * nkids, size)
    for c in range(nkids):
        out_ref[c] = strided(wide_ref, c, width, nkids, width)


def split(l2l):
    width, nkids, _ = l2l.shape
    return call(
        split_kernel,
        "split",
        jax.ShapeDtypeStruct((nkids, width, width), BF),
        [VMEM],
        [pltpu.VMEM((-(-width // 128), width * nkids, 128), F32)],
        24,
        1,
        4 * l2l.size,
    )(l2l)


def m2l_kernel(code_ref, extra_ref, part_ref, got_ref, core_ref, *rest):
    outs, (table_ref, acc_ref, z_ref) = rest[:4], rest[4:]
    here, me = lax.axis_index("dom"), lax.axis_index("sub")
    count, rank = part_ref.shape
    npart = got_ref.shape[0]
    offsets = core_ref.shape[0]
    table_ref[:, :rank] = part_ref[...]
    table_ref[:, rank:] = got_ref[:, :SURE, :].reshape(npart * SURE, rank)
    low = got_ref[pl.ds(jnp.maximum(here - 1, 0), 1), SURE:, :].reshape(SURE, rank)
    table_ref[pl.ds(pl.multiple_of(here * SURE, SURE), SURE), rank:] = low
    high = got_ref[pl.ds(jnp.minimum(here + 1, npart - 1), 1), SURE:, :].reshape(SURE, rank)
    none = jnp.zeros_like(high)
    tail = jnp.concatenate(
        [jnp.concatenate([high, none], axis=1), jnp.concatenate([none, high], axis=1)], axis=0
    )
    table = table_ref[...]
    lane = lax.broadcasted_iota(I32, (1, 128), 1)
    for k in range(0, offsets, 2):
        ks = range(k, min(k + 2, offsets))
        picked = []
        for kk in ks:
            code = jnp.broadcast_to(code_ref[:, kk:kk + 1], (count, 128))
            row = (code & 1023).astype(jnp.int16)
            hot = jnp.concatenate(
                [
                    jnp.where(row == (lane + base).astype(jnp.int16), BF(1), BF(0))
                    for base in range(0, count, 128)
                ],
                axis=1,
            )
            both = dot(hot, table)
            picked.append(jnp.where(code >= 1024, both[:, rank:], both[:, :rank]).astype(BF))
        n = len(picked)
        lhs = jnp.concatenate(
            [jnp.concatenate(picked, axis=1), tail[:n * SURE, :n * rank]], axis=0
        )
        both = dot(lhs, core_ref[k:k + n].reshape(n * rank, rank))
        z_ref[k * SURE:(k + n) * SURE, :] = both[count:].astype(BF)
        if k == 0:
            acc_ref[...] = both[:count]
        else:
            acc_ref[...] += both[:count]
    zrows = z_ref.shape[0]
    if zrows > offsets * SURE:
        z_ref[offsets * SURE:, :] = jnp.zeros((zrows - offsets * SURE, rank), BF)
    ahead = lax.broadcasted_iota(I32, (128, zrows), 0)
    group = lax.shift_right_logical(lax.broadcasted_iota(I32, (128, zrows), 1), 4)
    spread = dot(extra_ref[...], jnp.where(ahead == group, 1.0, 0.0).astype(BF))
    slot = (lax.broadcasted_iota(I32, (1, zrows), 1) & (SURE - 1)).astype(F32)
    hot = jnp.where(spread == slot, 1.0, 0.0).astype(BF)
    acc_ref[...] += dot(hot, z_ref[...])
    share = count // 4
    for shift, out in enumerate(outs):
        start = lax.rem(me + shift, 4) * share
        out[...] = acc_ref[pl.ds(pl.multiple_of(start, share), share), :].astype(out.dtype)


def m2l(code, extra, part, got, core):
    count, rank = part.shape
    offsets = core.shape[0]
    zrows = -(-offsets * SURE // 128) * 128
    piece = (count // 4, rank)
    return call(
        m2l_kernel,
        "m2l",
        tuple(jax.ShapeDtypeStruct(piece, BF if i else F32) for i in range(4)),
        [VMEM] * 5,
        [
            pltpu.VMEM((count, 2 * rank), BF),
            pltpu.VMEM((count, rank), F32),
            pltpu.VMEM((zrows, rank), BF),
        ],
        32,
        2 * count * offsets * rank * (2 * count + rank),
        2 * core.size,
    )(code, extra, part, got, core)


def down_kernel(own_ref, one_ref, two_ref, three_ref, expand_ref, l2l_ref, inh_ref, out_ref, rows_ref):
    nkids, width = l2l_ref.shape[0], l2l_ref.shape[1]
    count = own_ref.shape[0]
    acc = own_ref[...]
    for ref in (one_ref, two_ref, three_ref):
        acc = acc + ref[...].astype(F32)
    local = lax.dot_general(
        acc.astype(BF), expand_ref[...], (((1,), (1,)), ((), ())), preferred_element_type=F32
    ).astype(BF)
    for c in range(nkids):
        kid = dot(local, l2l_ref[c])
        kid = jnp.concatenate([kid, jnp.zeros((count, -width % 128), F32)], axis=1)
        for i in range(rows_ref.shape[0]):
            rows_ref[i, pl.ds(c, count, stride=nkids), :] = kid[:, i * 128:(i + 1) * 128]
    for j in range(out_ref.shape[1] // 128):
        cols = slice(j * 128, (j + 1) * 128)
        for i, base in enumerate(range(0, width, 128)):
            rows = slice(base, min(base + 128, width))
            far = rows_ref[i, cols, :].T[:rows.stop - base]
            out_ref[rows, cols] = (far + inh_ref[rows, cols].astype(F32)).astype(BF)


def downward(pieces, expand_t, l2l, inherited_t):
    nkids, width, _ = l2l.shape
    return call(
        down_kernel,
        "downward",
        jax.ShapeDtypeStruct(inherited_t.shape, BF),
        [VMEM] * 7,
        [pltpu.VMEM((-(-width // 128), inherited_t.shape[1], 128), F32)],
        32,
        2 * inherited_t.size * width,
        2 * (2 * inherited_t.size + l2l.size),
    )(*pieces, expand_t, l2l, inherited_t)


def local(leaf_mult, m2m, compress, m2l_core, expand, l2l, inherited, send_rows, m2l_list):
    npart, nsub = lax.axis_size("dom"), lax.axis_size("sub")

    def shifted(x, shift):
        return lax.ppermute(x, "sub", [(i, (i + shift) % nsub) for i in range(nsub)])

    packed = upward(leaf_mult.T, m2m, compress)
    pieces = [packed] + [shifted(packed, shift) for shift in (1, 2, 3)]
    code, extra = prepare(m2l_list.T)
    kids = split(l2l)
    part, send = pick(pieces, send_rows.reshape(npart * CAP, 1), npart)
    got = lax.all_to_all(send, "dom", 0, 0, tiled=True)
    sums = m2l(code, extra, part, got, m2l_core)
    sums = [sums[0]] + [shifted(sums[shift], shift) for shift in (1, 2, 3)]
    return downward(sums, expand.T, kids, inherited.T).T


def solution(mesh):
    placed = (
        P(("dom", "sub"), None),
        P(),
        P(),
        P("sub", None, None),
        P(),
        P(),
        P(("dom", "sub"), None),
        P("dom", None, None),
        P("dom", "sub"),
    )
    return jax.shard_map(
        local, mesh=mesh, in_specs=placed, out_specs=P(("dom", "sub"), None), check_vma=False
    )
```

time: 187 us -> 62.2 us (0.33); the launches traced: 185 us -> 62 us
  matrix products: 72.5 us -> 0 us
  blocking collectives: 41.1 us -> 0 us
  Pallas kernels: 0 us -> 27.1 us
  local copies, waits for them, and re-layouts: 23.2 us -> 4.79 us
  waiting for transfers between devices: 29.9 us -> 11.5 us
  starting transfers between devices: 0.04 us -> 18.4 us
  between operations: 13.6 us -> 0.12 us
  other arithmetic: 4.18 us -> 0 us
    dot_general x18 -> x0, matrix products: 72.5 us -> none  [the longest x8 54.1 us: one_block(): jnp.einsum('tkr,rd->tkd', onehot, table, preferred_element_type=jnp.float32)]
    all_gather x2 -> x0, blocking collectives: 41.1 us -> none  [the longest x1 29.8 us: local(): lists = lax.all_gather(send_rows, 'dom', axis=0, tiled=True)]
    pallas_call x0 -> x6, Pallas kernels: none -> 27.1 us  [the longest x1 15.7 us: m2l(): call(m2l_kernel, 'm2l', tuple((jax.ShapeDtypeStruct(piece, BF if i else F...]
    all_gather x1 -> x0, waiting for transfers between devices: 21.4 us -> none  [local(): everything = lax.all_gather(part_rows, 'dom', axis=0, tiled=True)]
    reshape x4 -> x1, local copies, waits for them, and re-layouts: 15.7 us -> 0.53 us  [local(): part, send = pick(pieces, send_rows.reshape(npart * CAP, 1), npart)]
    all_to_all x0 -> x1, starting transfers between devices: none -> 10.2 us  [local(): got = lax.all_to_all(send, 'dom', 0, 0, tiled=True)]
    all_to_all x0 -> x1, waiting for transfers between devices: none -> 8.49 us  [local(): got = lax.all_to_all(send, 'dom', 0, 0, tiled=True)]
    reduce_scatter x1 -> x0, waiting for transfers between devices: 8.49 us -> none  [local(): lax.psum_scatter(lax.map(one_block, listed).reshape(count, rank_width).as...]
  transfers between devices with their start and end apart: 2 -> 7, of which waited for: 2 -> 3; matrix products, arithmetic and copies ran while one was open for 5% -> 1% of each run, Pallas kernels for 0% -> 5%
where the time goes in v1:
time: 62.2 us; the launch traced here: 62 us
  Pallas kernels  27.1 us (44%)
  starting transfers between devices  18.4 us (30%)
  waiting for transfers between devices  11.5 us (18%)
  local copies, waits for them, and re-layouts  4.79 us (8%)
    pallas_call x1, Pallas kernels, m2l(): call(m2l_kernel, 'm2l', tuple((jax.ShapeDtypeStruct(piece, BF if i else F...  15.7 us
    all_to_all x1, starting transfers between devices, local(): got = lax.all_to_all(send, 'dom', 0, 0, tiled=True)  10.2 us
    all_to_all x1, waiting for transfers between devices, local(): got = lax.all_to_all(send, 'dom', 0, 0, tiled=True)  8.49 us
    ppermute x6, starting transfers between devices, shifted(): lax.ppermute(x, 'sub', [(i, (i + shift) % nsub) for i in range(nsub)])  8.2 us
    pallas_call x1, Pallas kernels, upward(): call(up_kernel, 'upward', jax.ShapeDtypeStruct((count, compress.shape[1])...  4.69 us
    unnamed x18, local copies, waits for them, and re-layouts  4.26 us
    ppermute x6, waiting for transfers between devices, shifted(): lax.ppermute(x, 'sub', [(i, (i + shift) % nsub) for i in range(nsub)])  3.04 us
    pallas_call x1, Pallas kernels, split(): call(split_kernel, 'split', jax.ShapeDtypeStruct((nkids, width, width), B...  2.71 us
  transfers between devices with their start and end apart: 7, of which 3 were waited for; matrix products, arithmetic and copies ran while one was open for 1% of the time, Pallas kernels for 5%

profile of v1, /device:TPU:1, one launch (start us, length us, event | category | flops | bytes accessed | tf_op | source)
XLA Modules:
  0.0 62.0 jit_solution(8279916705138394678)
XLA Ops:
  0.0 0.0 copy-start
  0.0 2.1 %copy-done = bf16[8,488,488]{2,1,0:T(8,128)(2,1)S(1)} copy-done((bf16[8,488,488]{2,1,0:T(8,128)(2,1)S(1)}, bf16[8,488,488]{2,1,0:T(8,128)(2,1)}, u32[]{:S(2)}) %copy-start) | copy-done | bytes 3810328
  2.1 0.0 copy-start.2
  2.1 1.2 %copy-done.2 = bf16[1024,488]{0,1:T(8,128)(2,1)S(1)} copy-done((bf16[1024,488]{0,1:T(8,128)(2,1)S(1)}, bf16[1024,488]{0,1:T(8,128)(2,1)}, u32[]{:S(2)}) %copy-start.2) | copy-done | bytes 999448
  3.3 0.0 copy-start.5
  3.3 0.9 %copy-done.5 = bf16[488,128]{1,0:T(8,128)(2,1)S(1)} copy-done((bf16[488,128]{1,0:T(8,128)(2,1)S(1)}, bf16[488,128]{1,0:T(8,128)(2,1)}, u32[]{:S(2)}) %copy-start.5) | copy-done | bytes 124952
  4.2 0.0 copy-start.8
  4.2 0.0 copy-start.4
  4.2 0.0 copy-start.7
  4.2 4.7 %upward.1.own_ref = bf16[128,128]{1,0:T(8,128)(2,1)S(1)} custom-call(bf16[488,1024]{1,0:T(8,128)(2,1)S(1)} %bitcast.5, bf16[8,488,488]{2,1,0:T(8,128)(2,1)S(1)} %copy-done, bf16[488,128]{1,0:T(8,128)(2,1)S(1)} %copy-done.5), custom_call_target="tpu_custom_call" | custom-call | flops 487718912 | bytes 4809728 | tf_op jit(solution)/shard_map/upward/pallas_call | solution.py:66
  8.9 3.6 %collective-permute-start.2 = (bf16[128,128]{1,0:T(8,128)(2,1)S(1)}, bf16[128,128]{1,0:T(8,128)(2,1)S(1)}, u32[]{:S(2)}, u32[]{:S(2)}) collective-permute-start(bf16[128,128]{1,0:T(8,128)(2,1)S(1)} %upward.1.own_ref), channel_id=1, source_target_pairs={{0,3},{1,0},{2,1},{3,2},{4,7},{5,4},{6,5},{7,6},{8,11},{9,8},{10,9... | collective-permute-start | bytes 98312 | tf_op jit(solution)/shard_map/ppermute | solution.py:297
  12.6 0.3 collective-permute-start.1
  12.9 0.7 %collective-permute-start = (bf16[128,128]{1,0:T(8,128)(2,1)S(1)}, bf16[128,128]{1,0:T(8,128)(2,1)S(1)}, u32[]{:S(2)}, u32[]{:S(2)}) collective-permute-start(bf16[128,128]{1,0:T(8,128)(2,1)S(1)} %upward.1.own_ref), channel_id=1, source_target_pairs={{0,1},{1,2},{2,3},{3,0},{4,5},{5,6},{6,7},{7,4},{8,9},{9,10},{10,1... | collective-permute-start | bytes 98312 | tf_op jit(solution)/shard_map/ppermute | solution.py:297
  13.6 0.0 copy-done.8
  13.6 0.5 reshape.4.rows_ref
  14.2 0.0 collective-permute-done.2.three_ref
  14.2 2.7 %collective-permute-done.1.two_ref = bf16[128,128]{1,0:T(8,128)(2,1)S(1)} collective-permute-done((bf16[128,128]{1,0:T(8,128)(2,1)S(1)}, bf16[128,128]{1,0:T(8,128)(2,1)S(1)}, u32[]{:S(2)}, u32[]{:S(2)}) %collective-permute-start.1) | collective-permute-done | bytes 32800 | tf_op jit(solution)/shard_map/ppermute | solution.py:297
  16.9 0.3 collective-permute-done.one_ref
  17.2 1.2 %pick.1 = (bf16[512,128]{1,0:T(8,128)(2,1)S(1)}, bf16[32,32,128]{2,1,0:T(8,128)(2,1)}) custom-call(bf16[128,128]{1,0:T(8,128)(2,1)S(1)} %upward.1.own_ref, bf16[128,128]{1,0:T(8,128)(2,1)S(1)} %collective-permute-done.one_ref, bf16[128,128]{1,0:T(8,128)(2,1)S(1)} %collective-permute-done.1.two_ref, bf16[128,128]{1,0:T(8,128)(2,1)S(1)} %collective-permute-done.2.three_ref, ...), custom_call_target="tpu_custom_call" | custom-call | flops 134217728 | bytes 262144 | tf_op jit(solution)/shard_map/pick/pallas_call | solution.py:104
  18.4 10.2 %all-to-all-start = ((bf16[32,32,128]{2,1,0:T(8,128)(2,1)}), bf16[32,32,128]{2,1,0:T(8,128)(2,1)S(1)}, u32[]{:S(2)}, u32[]{:S(2)}) async-start(bf16[32,32,128]{2,1,0:T(8,128)(2,1)} %get-tuple-element.16), calls=%async_computation | async-start | bytes 524288 | tf_op jit(solution)/shard_map/all_to_all | solution.py:304
  28.6 0.0 copy-done.4
  28.6 0.2 prepare.1
  28.8 8.5 %all-to-all-done.got_ref = bf16[32,32,128]{2,1,0:T(8,128)(2,1)S(1)} async-done(((bf16[32,32,128]{2,1,0:T(8,128)(2,1)}), bf16[32,32,128]{2,1,0:T(8,128)(2,1)S(1)}, u32[]{:S(2)}, u32[]{:S(2)}) %all-to-all-start) | async-done | bytes 262176 | tf_op jit(solution)/shard_map/all_to_all | solution.py:304
  37.3 0.0 copy-done.7
  37.3 0.0 copy-start.1
  37.3 15.7 %m2l.1 = (f32[128,128]{1,0:T(8,128)S(1)}, bf16[128,128]{1,0:T(8,128)(2,1)S(1)}, bf16[128,128]{1,0:T(8,128)(2,1)S(1)}, bf16[128,128]{1,0:T(8,128)(2,1)S(1)}) custom-call(s32[512,128]{1,0:T(8,128)S(1)} %get-tuple-element.13.code_ref, bf16[512,128]{1,0:T(8,128)(2,1)S(1)} %get-tuple-element.14.extra_ref, bf16[512,128]{1,0:T(8,128)(2,1)S(1)} %get-tuple-element.15.part_ref, ...), custom_call_target="tpu_custom_call" | custom-call | flops 11928600576 | bytes 2588672 | tf_op jit(solution)/shard_map/m2l/pallas_call | solution.py:241
  53.1 0.1 collective-permute-start.3
  53.1 1.5 %collective-permute-start.4 = (bf16[128,128]{1,0:T(8,128)(2,1)S(1)}, bf16[128,128]{1,0:T(8,128)(2,1)S(1)}, u32[]{:S(2)}, u32[]{:S(2)}) collective-permute-start(bf16[128,128]{1,0:T(8,128)(2,1)S(1)} %get-tuple-element.19), channel_id=1, source_target_pairs={{0,2},{1,3},{2,0},{3,1},{4,6},{5,7},{6,4},{7,5},{8,10},{9,11},{10,... | collective-permute-start | bytes 98312 | tf_op jit(solution)/shard_map/ppermute | solution.py:297
  54.6 0.0 copy-start.3
  54.6 0.0 copy-start.6
  54.6 2.0 %collective-permute-start.5 = (bf16[128,128]{1,0:T(8,128)(2,1)S(1)}, bf16[128,128]{1,0:T(8,128)(2,1)S(1)}, u32[]{:S(2)}, u32[]{:S(2)}) collective-permute-start(bf16[128,128]{1,0:T(8,128)(2,1)S(1)} %get-tuple-element.20), channel_id=1, source_target_pairs={{0,3},{1,0},{2,1},{3,2},{4,7},{5,4},{6,5},{7,6},{8,11},{9,8},{10,9... | collective-permute-start | bytes 98312 | tf_op jit(solution)/shard_map/ppermute | solution.py:297
  56.6 0.0 copy-done.1
  56.6 2.7 %split.1.l2l_ref = bf16[8,488,488]{2,1,0:T(8,128)(2,1)S(1)} custom-call(bf16[488,8,488]{2,1,0:T(8,128)(2,1)S(1)} %copy-done.1), custom_call_target="tpu_custom_call" | custom-call | flops 1 | bytes 7620608 | tf_op jit(solution)/shard_map/split/pallas_call | solution.py:167
  59.3 0.0 collective-permute-done.3.one_ref
  59.3 0.0 collective-permute-done.4.two_ref
  59.3 0.0 collective-permute-done.5.three_ref
  59.4 0.0 copy-done.3
  59.4 0.0 copy-done.6
  59.4 2.6 %downward.1 = bf16[488,1024]{1,0:T(8,128)(2,1)} custom-call(f32[128,128]{1,0:T(8,128)S(1)} %get-tuple-element.17.own_ref, bf16[128,128]{1,0:T(8,128)(2,1)S(1)} %collective-permute-done.3.one_ref, bf16[128,128]{1,0:T(8,128)(2,1)S(1)} %collective-permute-done.4.two_ref, bf16[128,128]{1,0:T(8,128)(2,1)S(1)} %collective-permute-done.5.three_ref, ...), custom_call_target="tpu_custom_call" | custom-call | flops 487718912 | bytes 5809152 | tf_op jit(solution)/shard_map/downward/pallas_call | solution.py:281
Async XLA Ops:
  0.0 2.1 %copy-start = (bf16[8,488,488]{2,1,0:T(8,128)(2,1)S(1)}, bf16[8,488,488]{2,1,0:T(8,128)(2,1)}, u32[]{:S(2)}) copy-start(bf16[8,488,488]{2,1,0:T(8,128)(2,1)} %m2m_ref.1) | copy-start | bytes 11430916
  2.1 1.2 %copy-start.2 = (bf16[1024,488]{0,1:T(8,128)(2,1)S(1)}, bf16[1024,488]{0,1:T(8,128)(2,1)}, u32[]{:S(2)}) copy-start(bf16[1024,488]{0,1:T(8,128)(2,1)} %param.9) | copy-start | bytes 2998276
  3.3 0.9 %copy-start.5 = (bf16[488,128]{1,0:T(8,128)(2,1)S(1)}, bf16[488,128]{1,0:T(8,128)(2,1)}, u32[]{:S(2)}) copy-start(bf16[488,128]{1,0:T(8,128)(2,1)} %compress_ref.1) | copy-start | bytes 374788
  4.2 9.4 %copy-start.8 = (s32[1,32,32]{2,1,0:T(8,128)S(1)}, s32[1,32,32]{2,1,0:T(8,128)}, u32[]{:S(2)}) copy-start(s32[1,32,32]{2,1,0:T(8,128)} %param.16) | copy-start | bytes 12292
  4.2 24.4 %copy-start.4 = (s32[512,79]{0,1:T(8,128)S(1)}, s32[512,79]{0,1:T(8,128)}, u32[]{:S(2)}) copy-start(s32[512,79]{0,1:T(8,128)} %param.17) | copy-start | bytes 485380
  4.2 33.1 %copy-start.7 = (bf16[79,128,128]{2,1,0:T(8,128)(2,1)S(1)}, bf16[79,128,128]{2,1,0:T(8,128)(2,1)}, u32[]{:S(2)}) copy-start(bf16[79,128,128]{2,1,0:T(8,128)(2,1)} %core_ref.1) | copy-start | bytes 7766020
  8.9 5.2 %collective-permute-start.2 = (bf16[128,128]{1,0:T(8,128)(2,1)S(1)}, bf16[128,128]{1,0:T(8,128)(2,1)S(1)}, u32[]{:S(2)}, u32[]{:S(2)}) collective-permute-start(bf16[128,128]{1,0:T(8,128)(2,1)S(1)} %upward.1.own_ref), channel_id=1, source_target_pairs={{0,3},{1,0},{2,1},{3,2},{4,7},{5,4},{6,5},{7,6},{8,11},{9,8},{10,9... | collective-permute-start | bytes 98312 | tf_op jit(solution)/shard_map/ppermute | solution.py:297
  12.6 4.3 %collective-permute-start.1 = (bf16[128,128]{1,0:T(8,128)(2,1)S(1)}, bf16[128,128]{1,0:T(8,128)(2,1)S(1)}, u32[]{:S(2)}, u32[]{:S(2)}) collective-permute-start(bf16[128,128]{1,0:T(8,128)(2,1)S(1)} %upward.1.own_ref), channel_id=1, source_target_pairs={{0,2},{1,3},{2,0},{3,1},{4,6},{5,7},{6,4},{7,5},{8,10},{9,11},{10,... | collective-permute-start | bytes 98312 | tf_op jit(solution)/shard_map/ppermute | solution.py:297
  12.9 4.3 %collective-permute-start = (bf16[128,128]{1,0:T(8,128)(2,1)S(1)}, bf16[128,128]{1,0:T(8,128)(2,1)S(1)}, u32[]{:S(2)}, u32[]{:S(2)}) collective-permute-start(bf16[128,128]{1,0:T(8,128)(2,1)S(1)} %upward.1.own_ref), channel_id=1, source_target_pairs={{0,1},{1,2},{2,3},{3,0},{4,5},{5,6},{6,7},{7,4},{8,9},{9,10},{10,1... | collective-permute-start | bytes 98312 | tf_op jit(solution)/shard_map/ppermute | solution.py:297
  18.4 18.9 %all-to-all-start = ((bf16[32,32,128]{2,1,0:T(8,128)(2,1)}), bf16[32,32,128]{2,1,0:T(8,128)(2,1)S(1)}, u32[]{:S(2)}, u32[]{:S(2)}) async-start(bf16[32,32,128]{2,1,0:T(8,128)(2,1)} %get-tuple-element.16), calls=%async_computation | async-start | bytes 524288 | tf_op jit(solution)/shard_map/all_to_all | solution.py:304
  37.3 19.3 %copy-start.1 = (bf16[488,8,488]{2,1,0:T(8,128)(2,1)S(1)}, bf16[488,8,488]{2,1,0:T(8,128)(2,1)}, u32[]{:S(2)}) copy-start(bf16[488,8,488]{2,1,0:T(8,128)(2,1)} %l2l_ref.1) | copy-start | bytes 11430916
  53.1 6.3 %collective-permute-start.3 = (bf16[128,128]{1,0:T(8,128)(2,1)S(1)}, bf16[128,128]{1,0:T(8,128)(2,1)S(1)}, u32[]{:S(2)}, u32[]{:S(2)}) collective-permute-start(bf16[128,128]{1,0:T(8,128)(2,1)S(1)} %get-tuple-element.18), channel_id=1, source_target_pairs={{0,1},{1,2},{2,3},{3,0},{4,5},{5,6},{6,7},{7,4},{8,9},{9,10},{10,1... | collective-permute-start | bytes 98312 | tf_op jit(solution)/shard_map/ppermute | solution.py:297
  53.1 6.2 %collective-permute-start.4 = (bf16[128,128]{1,0:T(8,128)(2,1)S(1)}, bf16[128,128]{1,0:T(8,128)(2,1)S(1)}, u32[]{:S(2)}, u32[]{:S(2)}) collective-permute-start(bf16[128,128]{1,0:T(8,128)(2,1)S(1)} %get-tuple-element.19), channel_id=1, source_target_pairs={{0,2},{1,3},{2,0},{3,1},{4,6},{5,7},{6,4},{7,5},{8,10},{9,11},{10,... | collective-permute-start | bytes 98312 | tf_op jit(solution)/shard_map/ppermute | solution.py:297
  54.6 4.7 %copy-start.3 = (bf16[1024,488]{0,1:T(8,128)(2,1)S(1)}, bf16[1024,488]{0,1:T(8,128)(2,1)}, u32[]{:S(2)}) copy-start(bf16[1024,488]{0,1:T(8,128)(2,1)} %param.15) | copy-start | bytes 2998276
  54.6 4.7 %copy-start.6 = (bf16[128,488]{0,1:T(8,128)(2,1)S(1)}, bf16[128,488]{0,1:T(8,128)(2,1)}, u32[]{:S(2)}) copy-start(bf16[128,488]{0,1:T(8,128)(2,1)} %param.13) | copy-start | bytes 374788
  54.6 4.7 %collective-permute-start.5 = (bf16[128,128]{1,0:T(8,128)(2,1)S(1)}, bf16[128,128]{1,0:T(8,128)(2,1)S(1)}, u32[]{:S(2)}, u32[]{:S(2)}) collective-permute-start(bf16[128,128]{1,0:T(8,128)(2,1)S(1)} %get-tuple-element.20), channel_id=1, source_target_pairs={{0,3},{1,0},{2,1},{3,2},{4,7},{5,4},{6,5},{7,6},{8,11},{9,8},{10,9... | collective-permute-start | bytes 98312 | tf_op jit(solution)/shard_map/ppermute | solution.py:297

commit v2 on v1

v2 whole, which is shorter than its diff:
```python
import jax
import jax.numpy as jnp
from jax import lax
from jax.experimental import pallas as pl
from jax.experimental.pallas import tpu as pltpu
from jax.sharding import PartitionSpec as P

BF = jnp.bfloat16
F32 = jnp.float32
I32 = jnp.int32
I16 = jnp.int16
MIB = 1 << 20
CAP = 32
SURE = 16
STEP = 2
HALF = 256

VMEM = pl.BlockSpec(memory_space=pltpu.VMEM)
HBM = pl.BlockSpec(memory_space=pltpu.HBM)


def dot(a, b):
    return jnp.dot(a, b, preferred_element_type=F32)


def call(kernel, name, out, ins, scratch, limit, flops, nbytes, place=VMEM):
    return pl.pallas_call(
        kernel,
        name=name,
        out_shape=out,
        in_specs=ins,
        out_specs=jax.tree.map(lambda _: place, out),
        scratch_shapes=scratch,
        compiler_params=pltpu.CompilerParams(vmem_limit_bytes=limit * MIB),
        cost_estimate=pl.CostEstimate(flops=flops, bytes_accessed=nbytes, transcendentals=0),
    )


def strided(ref, first, count, stride, width):
    parts = [ref[i, pl.ds(first, count, stride=stride), :] for i in range(ref.shape[0])]
    return jnp.concatenate(parts, axis=1)[:, :width].astype(BF)


def up_kernel(leaf_ref, m2m_ref, compress_ref, out_ref, leaf_buf, m2m_buf, compress_buf, rows_ref, sems):
    nkids, width = m2m_ref.shape[0], m2m_ref.shape[1]
    count = leaf_ref.shape[1] // nkids
    first = pltpu.make_async_copy(leaf_ref, leaf_buf, sems.at[nkids])
    copies = [
        pltpu.make_async_copy(m2m_ref.at[c], m2m_buf.at[c], sems.at[c]) for c in range(nkids)
    ]
    last = pltpu.make_async_copy(compress_ref, compress_buf, sems.at[nkids + 1])
    first.start()
    for copy in copies:
        copy.start()
    last.start()
    first.wait()
    for j in range(leaf_ref.shape[1] // 128):
        cols = slice(j * 128, (j + 1) * 128)
        for i, base in enumerate(range(0, width, 128)):
            size = min(128, width - base)
            rows_ref[i, cols, :size] = leaf_buf[base:base + size, cols].astype(F32).T
    total = jnp.zeros((count, width), F32)
    for c in range(nkids):
        kid = strided(rows_ref, c, count, nkids, width)
        copies[c].wait()
        total = total + dot(kid, m2m_buf[c])
    last.wait()
    out_ref[...] = dot(total.astype(BF), compress_buf[...]).astype(BF)


def upward(leaf_t, m2m, compress):
    nkids, width, _ = m2m.shape
    count = leaf_t.shape[1] // nkids
    return call(
        up_kernel,
        "upward",
        jax.ShapeDtypeStruct((count, compress.shape[1]), BF),
        [HBM] * 3,
        [
            pltpu.VMEM(leaf_t.shape, BF),
            pltpu.VMEM(m2m.shape, BF),
            pltpu.VMEM(compress.shape, BF),
            pltpu.VMEM((-(-width // 128), leaf_t.shape[1], 128), F32),
            pltpu.SemaphoreType.DMA((nkids + 2,)),
        ],
        60,
        2 * leaf_t.size * width,
        2 * (leaf_t.size + m2m.size),
    )(leaf_t, m2m, compress)


def one_hot(row, depth, first=0):
    lane = lax.broadcasted_iota(I32, (1, 128), 1)
    return jnp.concatenate(
        [
            jnp.where(row == (lane + (first + base)).astype(I16), BF(1), BF(0))
            for base in range(0, depth, 128)
        ],
        axis=1,
    )


def prep_kernel(list_ref, rows_ref, packed_ref, code_ref, hot_ref, own_ref):
    own_ref[...] = packed_ref[...]
    part = lax.axis_index("dom")
    offsets, count = list_ref.shape
    wanted = rows_ref.shape[0]
    hot_ref[...] = one_hot(jnp.broadcast_to(rows_ref[...], (wanted, 128)).astype(I16), count)
    value = list_ref[...]
    source = lax.shift_right_arithmetic(value - count, 5)
    slot = value & (CAP - 1)
    sure = slot < SURE
    row = jnp.where(sure, source * SURE + slot, part * SURE + slot - SURE)
    extra = ~sure & (source > part)
    code = jnp.where(extra, slot + (2 * count - SURE), row + count)
    code = jnp.where(value < count, value, code)
    code = jnp.concatenate([code, jnp.full((128 - offsets, count), -1, I32)], axis=0)
    for j in range(count // 128):
        cols = slice(j * 128, (j + 1) * 128)
        code_ref[cols, :] = code[:, cols].T.astype(I16)


def prepare(list_t, rows, packed):
    count = list_t.shape[1]
    return call(
        prep_kernel,
        "prepare",
        (
            jax.ShapeDtypeStruct((count, 128), I16),
            jax.ShapeDtypeStruct((rows.shape[0], count), BF),
            jax.ShapeDtypeStruct(packed.shape, BF),
        ),
        [VMEM] * 3,
        [],
        16,
        1,
        4 * list_t.size,
    )(list_t, rows, packed)


def pick_kernel(own_ref, one_ref, two_ref, three_ref, hot_ref, part_ref, send_ref):
    me = lax.axis_index("sub")
    count = own_ref.shape[0]
    for shift, ref in enumerate((own_ref, one_ref, two_ref, three_ref)):
        start = lax.rem(me + (4 - shift), 4) * count
        part_ref[pl.ds(pl.multiple_of(start, count), count), :] = ref[...]
    send_ref[...] = dot(hot_ref[...], part_ref[...]).astype(BF).reshape(send_ref.shape)


def pick(pieces, hot, npart):
    count, rank = pieces[0].shape
    return call(
        pick_kernel,
        "pick",
        (
            jax.ShapeDtypeStruct((4 * count, rank), BF),
            jax.ShapeDtypeStruct((npart, CAP, rank), BF),
        ),
        [VMEM] * 5,
        [],
        16,
        2 * hot.size * rank,
        2 * hot.size,
    )(*pieces, hot)


def split_kernel(l2l_ref, out_ref, wide_ref):
    width, nkids, _ = l2l_ref.shape
    for i, base in enumerate(range(0, width, 128)):
        size = min(128, width - base)
        block = l2l_ref[:, :, base:base + size].astype(F32)
        wide_ref[i, :, :size] = block.reshape(width * nkids, size)
    for c in range(nkids):
        out_ref[c] = strided(wide_ref, c, width, nkids, width)


def split(l2l):
    width, nkids, _ = l2l.shape
    return call(
        split_kernel,
        "split",
        jax.ShapeDtypeStruct((nkids, width, width), BF),
        [VMEM],
        [pltpu.VMEM((-(-width // 128), width * nkids, 128), F32)],
        24,
        1,
        4 * l2l.size,
    )(l2l)


def either(test, both):
    rank = both.shape[1] // 2
    return jnp.where(test != 0, both[:, rank:].astype(BF), both[:, :rank].astype(BF))


def accumulate(wide_ref, first, table_ref, core_ref, acc_ref):
    offsets, rank = core_ref.shape[0], core_ref.shape[1]
    table = table_ref[...]
    for k in range(0, offsets, STEP):
        n = min(STEP, offsets - k)
        lhs = []
        for i in range(k, k + n):
            code = jnp.broadcast_to(wide_ref[:, i:i + 1], wide_ref.shape).astype(I16)
            both = dot(one_hot(code & I16(~HALF), HALF, first), table)
            lhs.append(either(code & I16(HALF), both))
        core = core_ref[k:k + n].reshape(n * rank, rank)
        acc_ref[...] += dot(jnp.concatenate(lhs, axis=1), core)


def near_kernel(code_ref, part_ref, core_ref, acc_ref, table_ref, wide_ref):
    wide_ref[...] = code_ref[...].astype(I32)
    rank = part_ref.shape[1]
    table_ref[:, :rank] = part_ref[:HALF, :]
    table_ref[:, rank:] = part_ref[HALF:, :]
    acc_ref[...] = jnp.zeros_like(acc_ref)
    accumulate(wide_ref, 0, table_ref, core_ref, acc_ref)


def near(code, part, core):
    count, rank = part.shape
    return call(
        near_kernel,
        "near",
        jax.ShapeDtypeStruct((count, rank), F32),
        [VMEM] * 3,
        [pltpu.VMEM((HALF, 2 * rank), BF), pltpu.VMEM(code.shape, I32)],
        24,
        2 * count * core.shape[0] * rank * (count + rank),
        2 * core.size,
    )(code, part, core)


def far_kernel(code_ref, near_ref, got_ref, core_ref, *rest):
    outs, (table_ref, wide_ref, acc_ref, z_ref) = rest[:4], rest[4:]
    wide_ref[...] = code_ref[...].astype(I32)
    here, me = lax.axis_index("dom"), lax.axis_index("sub")
    npart, _, rank = got_ref.shape
    offsets = core_ref.shape[0]
    cut = npart // 2
    table_ref[:, :rank] = got_ref[:cut, :SURE, :].reshape(HALF, rank)
    table_ref[:, rank:] = got_ref[cut:, :SURE, :].reshape(HALF, rank)
    low = got_ref[pl.ds(jnp.maximum(here - 1, 0), 1), SURE:, :].reshape(SURE, rank)
    spot = pl.ds(pl.multiple_of(lax.rem(here, cut) * SURE, SURE), SURE)
    table_ref[spot, :rank] = jnp.where(here < cut, low, table_ref[spot, :rank])
    table_ref[spot, rank:] = jnp.where(here < cut, table_ref[spot, rank:], low)
    high = got_ref[pl.ds(jnp.minimum(here + 1, npart - 1), 1), SURE:, :].reshape(SURE, rank)
    none = jnp.zeros_like(high)
    tail = jnp.concatenate(
        [
            jnp.concatenate([none] * i + [high] + [none] * (STEP - 1 - i), axis=1)
            for i in range(STEP)
        ],
        axis=0,
    )
    zrows = z_ref.shape[0]
    z_ref[offsets * SURE:, :] = jnp.zeros((zrows - offsets * SURE, rank), BF)
    for k in range(0, offsets, STEP):
        n = min(STEP, offsets - k)
        core = core_ref[k:k + n].reshape(n * rank, rank)
        z_ref[k * SURE:(k + n) * SURE, :] = dot(tail[:n * SURE, :n * rank], core).astype(BF)
    slot = (lax.broadcasted_iota(I32, (1, zrows), 1) & (SURE - 1)).astype(F32) + 1.0
    ahead = lax.broadcasted_iota(I32, (128, zrows), 0)
    group = lax.shift_right_logical(lax.broadcasted_iota(I32, (128, zrows), 1), 4)
    spread = jnp.where(ahead == group, 1.0, 0.0).astype(BF)
    extra = jnp.maximum(wide_ref[...] - (4 * HALF - 1), 0).astype(F32).astype(BF)
    hot = jnp.where(dot(extra, spread) == slot, 1.0, 0.0).astype(BF)
    acc_ref[...] = near_ref[...] + dot(hot, z_ref[...])
    accumulate(wide_ref, 2 * HALF, table_ref, core_ref, acc_ref)
    share = acc_ref.shape[0] // 4
    for shift, out in enumerate(outs):
        start = lax.rem(me + shift, 4) * share
        out[...] = acc_ref[pl.ds(pl.multiple_of(start, share), share), :].astype(out.dtype)


def far(code, near_sums, got, core):
    count, rank = near_sums.shape
    offsets = core.shape[0]
    zrows = (offsets * SURE // 128 + 1) * 128
    piece = (count // 4, rank)
    return call(
        far_kernel,
        "far",
        tuple(jax.ShapeDtypeStruct(piece, BF if i else F32) for i in range(4)),
        [VMEM] * 4,
        [
            pltpu.VMEM((HALF, 2 * rank), BF),
            pltpu.VMEM(code.shape, I32),
            pltpu.VMEM((count, rank), F32),
            pltpu.VMEM((zrows, rank), BF),
        ],
        24,
        2 * count * offsets * rank * (count + rank),
        2 * core.size,
    )(code, near_sums, got, core)


def down_kernel(own_ref, one_ref, two_ref, three_ref, expand_ref, l2l_ref, inh_ref, out_ref, rows_ref):
    nkids, width = l2l_ref.shape[0], l2l_ref.shape[1]
    count = own_ref.shape[0]
    acc = own_ref[...]
    for ref in (one_ref, two_ref, three_ref):
        acc = acc + ref[...].astype(F32)
    local = lax.dot_general(
        acc.astype(BF), expand_ref[...], (((1,), (1,)), ((), ())), preferred_element_type=F32
    ).astype(BF)
    for c in range(nkids):
        kid = dot(local, l2l_ref[c])
        kid = jnp.concatenate([kid, jnp.zeros((count, -width % 128), F32)], axis=1)
        for i in range(rows_ref.shape[0]):
            rows_ref[i, pl.ds(c, count, stride=nkids), :] = kid[:, i * 128:(i + 1) * 128]
    for j in range(out_ref.shape[1] // 128):
        cols = slice(j * 128, (j + 1) * 128)
        for i, base in enumerate(range(0, width, 128)):
            rows = slice(base, min(base + 128, width))
            far = rows_ref[i, cols, :].T[:rows.stop - base]
            out_ref[rows, cols] = (far + inh_ref[rows, cols].astype(F32)).astype(BF)


def downward(pieces, expand_t, l2l, inherited_t):
    nkids, width, _ = l2l.shape
    return call(
        down_kernel,
        "downward",
        jax.ShapeDtypeStruct(inherited_t.shape, BF),
        [VMEM] * 7,
        [pltpu.VMEM((-(-width // 128), inherited_t.shape[1], 128), F32)],
        32,
        2 * inherited_t.size * width,
        2 * (2 * inherited_t.size + l2l.size),
    )(*pieces, expand_t, l2l, inherited_t)


def local(leaf_mult, m2m, compress, m2l_core, expand, l2l, inherited, send_rows, m2l_list):
    npart, nsub = lax.axis_size("dom"), lax.axis_size("sub")

    def shifted(x, shift):
        return lax.ppermute(x, "sub", [(i, (i + shift) % nsub) for i in range(nsub)])

    packed = upward(leaf_mult.T, m2m, compress)
    moved = [shifted(packed, shift) for shift in (1, 2, 3)]
    code, hot, own = prepare(m2l_list.T, send_rows.reshape(npart * CAP, 1), packed)
    kids = split(l2l)
    part, send = pick([own] + moved, hot, npart)
    got = lax.all_to_all(send, "dom", 0, 0, tiled=True)
    near_sums = near(code, part, m2l_core)
    sums = far(code, near_sums, got, m2l_core)
    sums = [sums[0]] + [shifted(sums[shift], shift) for shift in (1, 2, 3)]
    return downward(sums, expand.T, kids, inherited.T).T


def solution(mesh):
    placed = (
        P(("dom", "sub"), None),
        P(),
        P(),
        P("sub", None, None),
        P(),
        P(),
        P(("dom", "sub"), None),
        P("dom", None, None),
        P("dom", "sub"),
    )
    return jax.shard_map(
        local, mesh=mesh, in_specs=placed, out_specs=P(("dom", "sub"), None), check_vma=False
    )
```

time: 62.2 us -> 51.5 us (0.83)
  waiting for transfers between devices: 11.5 us -> 2.37 us
  local copies, waits for them, and re-layouts: 4.79 us -> 1.3 us
  Pallas kernels: 27.1 us -> 29 us
    all_to_all x1, waiting for transfers between devices: 8.49 us -> 0.25 us  [local(): got = lax.all_to_all(send, 'dom', 0, 0, tiled=True)]
    unnamed x18 -> x14, local copies, waits for them, and re-layouts: 4.26 us -> 0.78 us
    pallas_call x2 -> x3, Pallas kernels: 15.9 us -> 18.4 us  [the longest x1 9.59 us: far(): call(far_kernel, 'far', tuple((jax.ShapeDtypeStruct(piece, BF if i else F...]
    ppermute x6, waiting for transfers between devices: 3.04 us -> 2.12 us  [shifted(): lax.ppermute(x, 'sub', [(i, (i + shift) % nsub) for i in range(nsub)])]
  transfers between devices with their start and end apart: 7 -> 7, of which waited for: 3 -> 3; matrix products, arithmetic and copies ran while one was open for 1% -> 1% of each run, Pallas kernels for 5% -> 23%
where the time goes in v2:
time: 51.5 us; the launch traced here: 51.2 us
  Pallas kernels  29 us (56%)
  starting transfers between devices  18.4 us (36%)
  waiting for transfers between devices  2.37 us (5%)
  local copies, waits for them, and re-layouts  1.3 us (3%)
    all_to_all x1, starting transfers between devices, local(): got = lax.all_to_all(send, 'dom', 0, 0, tiled=True)  10.2 us
    pallas_call x1, Pallas kernels, far(): call(far_kernel, 'far', tuple((jax.ShapeDtypeStruct(piece, BF if i else F...  9.59 us
    pallas_call x1, Pallas kernels, near(): call(near_kernel, 'near', jax.ShapeDtypeStruct((count, rank), F32), [VMEM...  8.46 us
    ppermute x6, starting transfers between devices, shifted(): lax.ppermute(x, 'sub', [(i, (i + shift) % nsub) for i in range(nsub)])  8.21 us
    pallas_call x1, Pallas kernels, upward(): call(up_kernel, 'upward', jax.ShapeDtypeStruct((count, compress.shape[1])...  4.16 us
    pallas_call x1, Pallas kernels, split(): call(split_kernel, 'split', jax.ShapeDtypeStruct((nkids, width, width), B...  2.71 us
    pallas_call x1, Pallas kernels, downward(): call(down_kernel, 'downward', jax.ShapeDtypeStruct(inherited_t.shape, BF)...  2.59 us
    ppermute x6, waiting for transfers between devices, shifted(): lax.ppermute(x, 'sub', [(i, (i + shift) % nsub) for i in range(nsub)])  2.12 us
  transfers between devices with their start and end apart: 7, of which 3 were waited for; matrix products, arithmetic and copies ran while one was open for 1% of the time, Pallas kernels for 23%

profile of v2, /device:TPU:1, one launch (start us, length us, event | category | flops | bytes accessed | tf_op | source)
XLA Modules:
  0.0 51.2 jit_solution(12423193512518956745)
XLA Ops:
  0.0 0.0 copy-start.6
  0.0 0.0 copy-start.2
  0.0 0.0 copy-start.5
  0.0 4.2 %upward.1.packed_ref = bf16[128,128]{1,0:T(8,128)(2,1)} custom-call(bf16[488,1024]{1,0:T(8,128)(2,1)} %bitcast.8, bf16[8,488,488]{2,1,0:T(8,128)(2,1)} %m2m_ref.1, bf16[488,128]{1,0:T(8,128)(2,1)} %compress_ref.1), custom_call_target="tpu_custom_call" | custom-call | flops 487718912 | bytes 4809728 | tf_op jit(solution)/shard_map/upward/pallas_call | solution.py:74
  4.2 3.6 %collective-permute-start.2 = (bf16[128,128]{1,0:T(8,128)(2,1)}, bf16[128,128]{1,0:T(8,128)(2,1)S(1)}, u32[]{:S(2)}, u32[]{:S(2)}) collective-permute-start(bf16[128,128]{1,0:T(8,128)(2,1)} %upward.1.packed_ref), channel_id=1, source_target_pairs={{0,3},{1,0},{2,1},{3,2},{4,7},{5,4},{6,5},{7,6},{8,11},{9,8},{10,9... | collective-permute-start | bytes 98312 | tf_op jit(solution)/shard_map/ppermute | solution.py:337
  7.8 0.3 collective-permute-start.1
  8.2 0.7 %collective-permute-start = (bf16[128,128]{1,0:T(8,128)(2,1)}, bf16[128,128]{1,0:T(8,128)(2,1)S(1)}, u32[]{:S(2)}, u32[]{:S(2)}) collective-permute-start(bf16[128,128]{1,0:T(8,128)(2,1)} %upward.1.packed_ref), channel_id=1, source_target_pairs={{0,1},{1,2},{2,3},{3,0},{4,5},{5,6},{6,7},{7,4},{8,9},{9,10},{10,1... | collective-permute-start | bytes 98312 | tf_op jit(solution)/shard_map/ppermute | solution.py:337
  8.9 0.0 copy-done.6
  8.9 0.5 %reshape.4.rows_ref = s32[1024,1]{1,0:T(8,128)S(1)} reshape(s32[1,32,32]{2,1,0:T(8,128)S(1)} %copy-done.6) | data formatting | bytes 8192 | tf_op jit(solution)/shard_map/reshape | solution.py:341
  9.4 0.0 copy-done.2
  9.4 0.0 copy-start.3
  9.4 0.7 %copy-done.3 = bf16[128,128]{1,0:T(8,128)(2,1)S(1)} copy-done((bf16[128,128]{1,0:T(8,128)(2,1)S(1)}, bf16[128,128]{1,0:T(8,128)(2,1)}, u32[]{:S(2)}) %copy-start.3) | copy-done | bytes 32792
  10.2 0.3 prepare.1
  10.5 0.0 collective-permute-done.2.three_ref
  10.5 1.8 %collective-permute-done.1.two_ref = bf16[128,128]{1,0:T(8,128)(2,1)S(1)} collective-permute-done((bf16[128,128]{1,0:T(8,128)(2,1)}, bf16[128,128]{1,0:T(8,128)(2,1)S(1)}, u32[]{:S(2)}, u32[]{:S(2)}) %collective-permute-start.1) | collective-permute-done | bytes 32800 | tf_op jit(solution)/shard_map/ppermute | solution.py:337
  12.3 0.3 collective-permute-done.one_ref
  12.6 1.2 %pick.1 = (bf16[512,128]{1,0:T(8,128)(2,1)S(1)}, bf16[32,32,128]{2,1,0:T(8,128)(2,1)}) custom-call(bf16[128,128]{1,0:T(8,128)(2,1)S(1)} %get-tuple-element.15.own_ref, bf16[128,128]{1,0:T(8,128)(2,1)S(1)} %collective-permute-done.one_ref, bf16[128,128]{1,0:T(8,128)(2,1)S(1)} %collective-permute-done.1.two_ref, ...), custom_call_target="tpu_custom_call" | custom-call | flops 134217728 | bytes 1048576 | tf_op jit(solution)/shard_map/pick/pallas_call | solution.py:152
  13.8 10.2 %all-to-all-start = ((bf16[32,32,128]{2,1,0:T(8,128)(2,1)}), bf16[32,32,128]{2,1,0:T(8,128)(2,1)S(1)}, u32[]{:S(2)}, u32[]{:S(2)}) async-start(bf16[32,32,128]{2,1,0:T(8,128)(2,1)} %get-tuple-element.18), calls=%async_computation | async-start | bytes 524288 | tf_op jit(solution)/shard_map/all_to_all | solution.py:344
  24.0 0.0 copy-done.5
  24.0 8.5 %near.1.near_ref = f32[512,128]{1,0:T(8,128)S(1)} custom-call(s16[512,128]{1,0:T(8,128)(2,1)S(1)} %get-tuple-element.14.code_ref, bf16[512,128]{1,0:T(8,128)(2,1)S(1)} %get-tuple-element.17.part_ref, bf16[79,128,128]{2,1,0:T(8,128)(2,1)S(1)} %copy-done.5), custom_call_target="tpu_custom_call" | custom-call | flops 6627000320 | bytes 2588672 | tf_op jit(solution)/shard_map/near/pallas_call | solution.py:221
  32.5 0.2 all-to-all-done.got_ref
  32.7 0.0 copy-start
  32.7 9.6 %far.1 = (f32[128,128]{1,0:T(8,128)S(1)}, bf16[128,128]{1,0:T(8,128)(2,1)S(1)}, bf16[128,128]{1,0:T(8,128)(2,1)S(1)}, bf16[128,128]{1,0:T(8,128)(2,1)S(1)}) custom-call(s16[512,128]{1,0:T(8,128)(2,1)S(1)} %get-tuple-element.14.code_ref, f32[512,128]{1,0:T(8,128)S(1)} %near.1.near_ref, bf16[32,32,128]{2,1,0:T(8,128)(2,1)S(1)} %all-to-all-done.got_ref, ...), custom_call_target="tpu_custom_call" | custom-call | flops 6627000320 | bytes 2588672 | tf_op jit(solution)/shard_map/far/pallas_call | solution.py:280
  42.3 0.1 collective-permute-start.3
  42.4 1.5 %collective-permute-start.4 = (bf16[128,128]{1,0:T(8,128)(2,1)S(1)}, bf16[128,128]{1,0:T(8,128)(2,1)S(1)}, u32[]{:S(2)}, u32[]{:S(2)}) collective-permute-start(bf16[128,128]{1,0:T(8,128)(2,1)S(1)} %get-tuple-element.21), channel_id=1, source_target_pairs={{0,2},{1,3},{2,0},{3,1},{4,6},{5,7},{6,4},{7,5},{8,10},{9,11},{10,... | collective-permute-start | bytes 98312 | tf_op jit(solution)/shard_map/ppermute | solution.py:337
  43.9 0.0 copy-start.1
  43.9 0.0 copy-start.4
  43.9 2.0 %collective-permute-start.5 = (bf16[128,128]{1,0:T(8,128)(2,1)S(1)}, bf16[128,128]{1,0:T(8,128)(2,1)S(1)}, u32[]{:S(2)}, u32[]{:S(2)}) collective-permute-start(bf16[128,128]{1,0:T(8,128)(2,1)S(1)} %get-tuple-element.22), channel_id=1, source_target_pairs={{0,3},{1,0},{2,1},{3,2},{4,7},{5,4},{6,5},{7,6},{8,11},{9,8},{10,9... | collective-permute-start | bytes 98312 | tf_op jit(solution)/shard_map/ppermute | solution.py:337
  45.9 0.0 copy-done
  45.9 2.7 %split.1.l2l_ref = bf16[8,488,488]{2,1,0:T(8,128)(2,1)S(1)} custom-call(bf16[488,8,488]{2,1,0:T(8,128)(2,1)S(1)} %copy-done), custom_call_target="tpu_custom_call" | custom-call | flops 1 | bytes 7620608 | tf_op jit(solution)/shard_map/split/pallas_call | solution.py:179
  48.6 0.0 collective-permute-done.3.one_ref
  48.6 0.0 collective-permute-done.4.two_ref
  48.6 0.0 collective-permute-done.5.three_ref
  48.6 0.0 copy-done.1
  48.6 0.0 copy-done.4
  48.7 2.6 %downward.1 = bf16[488,1024]{1,0:T(8,128)(2,1)} custom-call(f32[128,128]{1,0:T(8,128)S(1)} %get-tuple-element.19.own_ref, bf16[128,128]{1,0:T(8,128)(2,1)S(1)} %collective-permute-done.3.one_ref, bf16[128,128]{1,0:T(8,128)(2,1)S(1)} %collective-permute-done.4.two_ref, bf16[128,128]{1,0:T(8,128)(2,1)S(1)} %collective-permute-done.5.three_ref, ...), custom_call_target="tpu_custom_call" | custom-call | flops 487718912 | bytes 5809152 | tf_op jit(solution)/shard_map/downward/pallas_call | solution.py:321
Async XLA Ops:
  0.0 8.9 %copy-start.6 = (s32[1,32,32]{2,1,0:T(8,128)S(1)}, s32[1,32,32]{2,1,0:T(8,128)}, u32[]{:S(2)}) copy-start(s32[1,32,32]{2,1,0:T(8,128)} %param.16) | copy-start | bytes 12292
  0.0 9.4 %copy-start.2 = (s32[512,79]{0,1:T(8,128)S(1)}, s32[512,79]{0,1:T(8,128)}, u32[]{:S(2)}) copy-start(s32[512,79]{0,1:T(8,128)} %param.17) | copy-start | bytes 485380
  0.0 24.0 %copy-start.5 = (bf16[79,128,128]{2,1,0:T(8,128)(2,1)S(1)}, bf16[79,128,128]{2,1,0:T(8,128)(2,1)}, u32[]{:S(2)}) copy-start(bf16[79,128,128]{2,1,0:T(8,128)(2,1)} %core_ref.3) | copy-start | bytes 7766020
  4.2 6.4 %collective-permute-start.2 = (bf16[128,128]{1,0:T(8,128)(2,1)}, bf16[128,128]{1,0:T(8,128)(2,1)S(1)}, u32[]{:S(2)}, u32[]{:S(2)}) collective-permute-start(bf16[128,128]{1,0:T(8,128)(2,1)} %upward.1.packed_ref), channel_id=1, source_target_pairs={{0,3},{1,0},{2,1},{3,2},{4,7},{5,4},{6,5},{7,6},{8,11},{9,8},{10,9... | collective-permute-start | bytes 98312 | tf_op jit(solution)/shard_map/ppermute | solution.py:337
  7.8 4.5 %collective-permute-start.1 = (bf16[128,128]{1,0:T(8,128)(2,1)}, bf16[128,128]{1,0:T(8,128)(2,1)S(1)}, u32[]{:S(2)}, u32[]{:S(2)}) collective-permute-start(bf16[128,128]{1,0:T(8,128)(2,1)} %upward.1.packed_ref), channel_id=1, source_target_pairs={{0,2},{1,3},{2,0},{3,1},{4,6},{5,7},{6,4},{7,5},{8,10},{9,11},{10,... | collective-permute-start | bytes 98312 | tf_op jit(solution)/shard_map/ppermute | solution.py:337
  8.2 4.5 %collective-permute-start = (bf16[128,128]{1,0:T(8,128)(2,1)}, bf16[128,128]{1,0:T(8,128)(2,1)S(1)}, u32[]{:S(2)}, u32[]{:S(2)}) collective-permute-start(bf16[128,128]{1,0:T(8,128)(2,1)} %upward.1.packed_ref), channel_id=1, source_target_pairs={{0,1},{1,2},{2,3},{3,0},{4,5},{5,6},{6,7},{7,4},{8,9},{9,10},{10,1... | collective-permute-start | bytes 98312 | tf_op jit(solution)/shard_map/ppermute | solution.py:337
  9.4 0.8 %copy-start.3 = (bf16[128,128]{1,0:T(8,128)(2,1)S(1)}, bf16[128,128]{1,0:T(8,128)(2,1)}, u32[]{:S(2)}) copy-start(bf16[128,128]{1,0:T(8,128)(2,1)} %upward.1.packed_ref) | copy-start | bytes 98308
  13.8 18.9 %all-to-all-start = ((bf16[32,32,128]{2,1,0:T(8,128)(2,1)}), bf16[32,32,128]{2,1,0:T(8,128)(2,1)S(1)}, u32[]{:S(2)}, u32[]{:S(2)}) async-start(bf16[32,32,128]{2,1,0:T(8,128)(2,1)} %get-tuple-element.18), calls=%async_computation | async-start | bytes 524288 | tf_op jit(solution)/shard_map/all_to_all | solution.py:344
  32.7 13.1 %copy-start = (bf16[488,8,488]{2,1,0:T(8,128)(2,1)S(1)}, bf16[488,8,488]{2,1,0:T(8,128)(2,1)}, u32[]{:S(2)}) copy-start(bf16[488,8,488]{2,1,0:T(8,128)(2,1)} %l2l_ref.1) | copy-start | bytes 11430916
  42.3 6.3 %collective-permute-start.3 = (bf16[128,128]{1,0:T(8,128)(2,1)S(1)}, bf16[128,128]{1,0:T(8,128)(2,1)S(1)}, u32[]{:S(2)}, u32[]{:S(2)}) collective-permute-start(bf16[128,128]{1,0:T(8,128)(2,1)S(1)} %get-tuple-element.20), channel_id=1, source_target_pairs={{0,1},{1,2},{2,3},{3,0},{4,5},{5,6},{6,7},{7,4},{8,9},{9,10},{10,1... | collective-permute-start | bytes 98312 | tf_op jit(solution)/shard_map/ppermute | solution.py:337
  42.4 6.2 %collective-permute-start.4 = (bf16[128,128]{1,0:T(8,128)(2,1)S(1)}, bf16[128,128]{1,0:T(8,128)(2,1)S(1)}, u32[]{:S(2)}, u32[]{:S(2)}) collective-permute-start(bf16[128,128]{1,0:T(8,128)(2,1)S(1)} %get-tuple-element.21), channel_id=1, source_target_pairs={{0,2},{1,3},{2,0},{3,1},{4,6},{5,7},{6,4},{7,5},{8,10},{9,11},{10,... | collective-permute-start | bytes 98312 | tf_op jit(solution)/shard_map/ppermute | solution.py:337
  43.9 4.7 %copy-start.1 = (bf16[1024,488]{0,1:T(8,128)(2,1)S(1)}, bf16[1024,488]{0,1:T(8,128)(2,1)}, u32[]{:S(2)}) copy-start(bf16[1024,488]{0,1:T(8,128)(2,1)} %param.15) | copy-start | bytes 2998276
  43.9 4.7 %copy-start.4 = (bf16[128,488]{0,1:T(8,128)(2,1)S(1)}, bf16[128,488]{0,1:T(8,128)(2,1)}, u32[]{:S(2)}) copy-start(bf16[128,488]{0,1:T(8,128)(2,1)} %param.13) | copy-start | bytes 374788
  43.9 4.7 %collective-permute-start.5 = (bf16[128,128]{1,0:T(8,128)(2,1)S(1)}, bf16[128,128]{1,0:T(8,128)(2,1)S(1)}, u32[]{:S(2)}, u32[]{:S(2)}) collective-permute-start(bf16[128,128]{1,0:T(8,128)(2,1)S(1)} %get-tuple-element.22), channel_id=1, source_target_pairs={{0,3},{1,0},{2,1},{3,2},{4,7},{5,4},{6,5},{7,6},{8,11},{9,8},{10,9... | collective-permute-start | bytes 98312 | tf_op jit(solution)/shard_map/ppermute | solution.py:337

commit v3 on v2

--- a/solution.py
+++ b/solution.py
@@ -12,8 +12,9 @@
 MIB = 1 << 20
 CAP = 32
 SURE = 16
-STEP = 2
+STEP = 4
 HALF = 256
+PITCH = 9
 
 VMEM = pl.BlockSpec(memory_space=pltpu.VMEM)
 HBM = pl.BlockSpec(memory_space=pltpu.HBM)
@@ -36,8 +37,8 @@
     )
 
 
-def strided(ref, first, count, stride, width):
-    parts = [ref[i, pl.ds(first, count, stride=stride), :] for i in range(ref.shape[0])]
+def kid_rows(ref, kid, count, width):
+    parts = [ref[i, pl.ds(kid, count, stride=PITCH), :] for i in range(ref.shape[0])]
     return jnp.concatenate(parts, axis=1)[:, :width].astype(BF)
 
 
@@ -58,10 +59,13 @@
         cols = slice(j * 128, (j + 1) * 128)
         for i, base in enumerate(range(0, width, 128)):
             size = min(128, width - base)
-            rows_ref[i, cols, :size] = leaf_buf[base:base + size, cols].astype(F32).T
+            turned = leaf_buf[base:base + size, cols].astype(F32).T
+            for o in range(0, 128, nkids):
+                at = (j * 128 + o) // nkids * PITCH
+                rows_ref[i, at:at + nkids, :size] = turned[o:o + nkids]
     total = jnp.zeros((count, width), F32)
     for c in range(nkids):
-        kid = strided(rows_ref, c, count, nkids, width)
+        kid = kid_rows(rows_ref, c, count, width)
         copies[c].wait()
         total = total + dot(kid, m2m_buf[c])
     last.wait()
@@ -80,7 +84,7 @@
             pltpu.VMEM(leaf_t.shape, BF),
             pltpu.VMEM(m2m.shape, BF),
             pltpu.VMEM(compress.shape, BF),
-            pltpu.VMEM((-(-width // 128), leaf_t.shape[1], 128), F32),
+            pltpu.VMEM((-(-width // 128), count * PITCH, 128), F32),
             pltpu.SemaphoreType.DMA((nkids + 2,)),
         ],
         60,
@@ -169,9 +173,10 @@
     for i, base in enumerate(range(0, width, 128)):
         size = min(128, width - base)
         block = l2l_ref[:, :, base:base + size].astype(F32)
-        wide_ref[i, :, :size] = block.reshape(width * nkids, size)
+        for p in range(width):
+            wide_ref[i, p * PITCH:p * PITCH + nkids, :size] = block[p]
     for c in range(nkids):
-        out_ref[c] = strided(wide_ref, c, width, nkids, width)
+        out_ref[c] = kid_rows(wide_ref, c, width, width)
 
 
 def split(l2l):
@@ -181,7 +186,7 @@
         "split",
         jax.ShapeDtypeStruct((nkids, width, width), BF),
         [VMEM],
-        [pltpu.VMEM((-(-width // 128), width * nkids, 128), F32)],
+        [pltpu.VMEM((-(-width // 128), width * PITCH, 128), F32)],
         24,
         1,
         4 * l2l.size,
@@ -193,9 +198,14 @@
     return jnp.where(test != 0, both[:, rank:].astype(BF), both[:, :rank].astype(BF))
 
 
-def accumulate(wide_ref, first, table_ref, core_ref, acc_ref):
+def accumulate(wide_ref, first, table_ref, core_ref, acc_ref, z_ref=None):
     offsets, rank = core_ref.shape[0], core_ref.shape[1]
     table = table_ref[...]
+    lane = lax.broadcasted_iota(I32, (1, 128), 1)
+    owner = lax.shift_right_logical(lane, 4).astype(I16)
+    wanted = ((lane & (SURE - 1)) + 4 * HALF).astype(I16)
+    per = 128 // SURE
+    mixed, hots = None, []
     for k in range(0, offsets, STEP):
         n = min(STEP, offsets - k)
         lhs = []
@@ -203,8 +213,17 @@
             code = jnp.broadcast_to(wide_ref[:, i:i + 1], wide_ref.shape).astype(I16)
             both = dot(one_hot(code & I16(~HALF), HALF, first), table)
             lhs.append(either(code & I16(HALF), both))
+            if z_ref is None:
+                continue
+            mixed = code if i % per == 0 else jnp.where(owner == I16(i % per), code, mixed)
+            if i % per == per - 1 or i == offsets - 1:
+                hots.append(jnp.where(mixed == wanted, BF(1), BF(0)))
         core = core_ref[k:k + n].reshape(n * rank, rank)
         acc_ref[...] += dot(jnp.concatenate(lhs, axis=1), core)
+        if len(hots) == 2 or (hots and k + n == offsets):
+            rows = pl.ds((k + n - 1) // (2 * per) * 256, 128 * len(hots))
+            acc_ref[...] += dot(jnp.concatenate(hots, axis=1), z_ref[rows, :])
+            hots = []
 
 
 def near_kernel(code_ref, part_ref, core_ref, acc_ref, table_ref, wide_ref):
@@ -258,14 +277,8 @@
         n = min(STEP, offsets - k)
         core = core_ref[k:k + n].reshape(n * rank, rank)
         z_ref[k * SURE:(k + n) * SURE, :] = dot(tail[:n * SURE, :n * rank], core).astype(BF)
-    slot = (lax.broadcasted_iota(I32, (1, zrows), 1) & (SURE - 1)).astype(F32) + 1.0
-    ahead = lax.broadcasted_iota(I32, (128, zrows), 0)
-    group = lax.shift_right_logical(lax.broadcasted_iota(I32, (128, zrows), 1), 4)
-    spread = jnp.where(ahead == group, 1.0, 0.0).astype(BF)
-    extra = jnp.maximum(wide_ref[...] - (4 * HALF - 1), 0).astype(F32).astype(BF)
-    hot = jnp.where(dot(extra, spread) == slot, 1.0, 0.0).astype(BF)
-    acc_ref[...] = near_ref[...] + dot(hot, z_ref[...])
-    accumulate(wide_ref, 2 * HALF, table_ref, core_ref, acc_ref)
+    acc_ref[...] = near_ref[...]
+    accumulate(wide_ref, 2 * HALF, table_ref, core_ref, acc_ref, z_ref)
     share = acc_ref.shape[0] // 4
     for shift, out in enumerate(outs):
         start = lax.rem(me + shift, 4) * share
@@ -294,7 +307,7 @@
     )(code, near_sums, got, core)
 
 
-def down_kernel(own_ref, one_ref, two_ref, three_ref, expand_ref, l2l_ref, inh_ref, out_ref, rows_ref):
+def down_kernel(own_ref, one_ref, two_ref, three_ref, expand_ref, l2l_ref, inh_ref, out_hbm, rows_ref, out_ref, sems):
     nkids, width = l2l_ref.shape[0], l2l_ref.shape[1]
     count = own_ref.shape[0]
     acc = own_ref[...]
@@ -307,26 +320,45 @@
         kid = dot(local, l2l_ref[c])
         kid = jnp.concatenate([kid, jnp.zeros((count, -width % 128), F32)], axis=1)
         for i in range(rows_ref.shape[0]):
-            rows_ref[i, pl.ds(c, count, stride=nkids), :] = kid[:, i * 128:(i + 1) * 128]
-    for j in range(out_ref.shape[1] // 128):
-        cols = slice(j * 128, (j + 1) * 128)
-        for i, base in enumerate(range(0, width, 128)):
-            rows = slice(base, min(base + 128, width))
-            far = rows_ref[i, cols, :].T[:rows.stop - base]
+            rows_ref[i, pl.ds(c, count, stride=PITCH), :] = kid[:, i * 128:(i + 1) * 128]
+    copies = []
+    for i, base in enumerate(range(0, width, 128)):
+        rows = slice(base, min(base + 128, width))
+        for j in range(out_ref.shape[1] // 128):
+            cols = slice(j * 128, (j + 1) * 128)
+            first = j * 128 // nkids
+            far = jnp.concatenate(
+                [
+                    rows_ref[i, o * PITCH:o * PITCH + nkids, :]
+                    for o in range(first, first + 128 // nkids)
+                ],
+                axis=0,
+            ).T[:rows.stop - base]
             out_ref[rows, cols] = (far + inh_ref[rows, cols].astype(F32)).astype(BF)
+        part = pl.ds(base, rows.stop - base)
+        copies.append(pltpu.make_async_copy(out_ref.at[part], out_hbm.at[part], sems.at[i]))
+        copies[-1].start()
+    for copy in copies:
+        copy.wait()
 
 
 def downward(pieces, expand_t, l2l, inherited_t):
     nkids, width, _ = l2l.shape
+    blocks = -(-width // 128)
     return call(
         down_kernel,
         "downward",
         jax.ShapeDtypeStruct(inherited_t.shape, BF),
         [VMEM] * 7,
-        [pltpu.VMEM((-(-width // 128), inherited_t.shape[1], 128), F32)],
+        [
+            pltpu.VMEM((blocks, pieces[0].shape[0] * PITCH, 128), F32),
+            pltpu.VMEM(inherited_t.shape, BF),
+            pltpu.SemaphoreType.DMA((blocks,)),
+        ],
         32,
         2 * inherited_t.size * width,
         2 * (2 * inherited_t.size + l2l.size),
+        HBM,
     )(*pieces, expand_t, l2l, inherited_t)
 
 

time: 51.5 us -> 49.7 us (0.965)
  Pallas kernels: 29 us -> 26.4 us
  waiting for transfers between devices: 2.37 us -> 3.06 us
    pallas_call x1, Pallas kernels: 2.71 us -> 1.08 us  [split(): call(split_kernel, 'split', jax.ShapeDtypeStruct((nkids, width, width), B...]
    ppermute x6, waiting for transfers between devices: 2.12 us -> 2.73 us  [shifted(): lax.ppermute(x, 'sub', [(i, (i + shift) % nsub) for i in range(nsub)])]
  transfers between devices with their start and end apart: 7 -> 7, of which waited for: 3 -> 4; matrix products, arithmetic and copies ran while one was open for 1% -> 1% of each run, Pallas kernels for 23% -> 20%
where the time goes in v3:
time: 49.7 us; the launch traced here: 49.5 us
  Pallas kernels  26.4 us (53%)
  starting transfers between devices  18.4 us (37%)
  waiting for transfers between devices  3.06 us (6%)
  local copies, waits for them, and re-layouts  1.3 us (3%)
    all_to_all x1, starting transfers between devices, local(): got = lax.all_to_all(send, 'dom', 0, 0, tiled=True)  10.2 us
    pallas_call x1, Pallas kernels, far(): call(far_kernel, 'far', tuple((jax.ShapeDtypeStruct(piece, BF if i else F...  9.41 us
    pallas_call x1, Pallas kernels, near(): call(near_kernel, 'near', jax.ShapeDtypeStruct((count, rank), F32), [VMEM...  8.38 us
    ppermute x6, starting transfers between devices, shifted(): lax.ppermute(x, 'sub', [(i, (i + shift) % nsub) for i in range(nsub)])  8.2 us
    pallas_call x1, Pallas kernels, upward(): call(up_kernel, 'upward', jax.ShapeDtypeStruct((count, compress.shape[1])...  3.74 us
    ppermute x6, waiting for transfers between devices, shifted(): lax.ppermute(x, 'sub', [(i, (i + shift) % nsub) for i in range(nsub)])  2.73 us
    pallas_call x1, Pallas kernels, downward(): call(down_kernel, 'downward', jax.ShapeDtypeStruct(inherited_t.shape, BF)...  2.27 us
    pallas_call x1, Pallas kernels, pick(): call(pick_kernel, 'pick', (jax.ShapeDtypeStruct((4 * count, rank), BF), j...  1.15 us
  transfers between devices with their start and end apart: 7, of which 4 were waited for; matrix products, arithmetic and copies ran while one was open for 1% of the time, Pallas kernels for 20%

profile of v3, /device:TPU:1, one launch (start us, length us, event | category | flops | bytes accessed | tf_op | source)
XLA Modules:
  0.0 49.5 jit_solution(10327541205114657950)
XLA Ops:
  0.0 0.0 copy-start.6
  0.0 0.0 copy-start.2
  0.0 0.0 copy-start.5
  0.0 3.7 %upward.1.packed_ref = bf16[128,128]{1,0:T(8,128)(2,1)} custom-call(bf16[488,1024]{1,0:T(8,128)(2,1)} %bitcast.8, bf16[8,488,488]{2,1,0:T(8,128)(2,1)} %m2m_ref.1, bf16[488,128]{1,0:T(8,128)(2,1)} %compress_ref.1), custom_call_target="tpu_custom_call" | custom-call | flops 487718912 | bytes 4809728 | tf_op jit(solution)/shard_map/upward/pallas_call | solution.py:78
  3.8 3.6 %collective-permute-start.2 = (bf16[128,128]{1,0:T(8,128)(2,1)}, bf16[128,128]{1,0:T(8,128)(2,1)S(1)}, u32[]{:S(2)}, u32[]{:S(2)}) collective-permute-start(bf16[128,128]{1,0:T(8,128)(2,1)} %upward.1.packed_ref), channel_id=1, source_target_pairs={{0,3},{1,0},{2,1},{3,2},{4,7},{5,4},{6,5},{7,6},{8,11},{9,8},{10,9... | collective-permute-start | bytes 98312 | tf_op jit(solution)/shard_map/ppermute | solution.py:369
  7.4 0.3 collective-permute-start.1
  7.7 0.7 %collective-permute-start = (bf16[128,128]{1,0:T(8,128)(2,1)}, bf16[128,128]{1,0:T(8,128)(2,1)S(1)}, u32[]{:S(2)}, u32[]{:S(2)}) collective-permute-start(bf16[128,128]{1,0:T(8,128)(2,1)} %upward.1.packed_ref), channel_id=1, source_target_pairs={{0,1},{1,2},{2,3},{3,0},{4,5},{5,6},{6,7},{7,4},{8,9},{9,10},{10,1... | collective-permute-start | bytes 98312 | tf_op jit(solution)/shard_map/ppermute | solution.py:369
  8.4 0.0 copy-done.6
  8.4 0.5 %reshape.4.rows_ref = s32[1024,1]{1,0:T(8,128)S(1)} reshape(s32[1,32,32]{2,1,0:T(8,128)S(1)} %copy-done.6) | data formatting | bytes 8192 | tf_op jit(solution)/shard_map/reshape | solution.py:373
  9.0 0.0 copy-done.2
  9.0 0.0 copy-start.3
  9.0 0.7 %copy-done.3 = bf16[128,128]{1,0:T(8,128)(2,1)S(1)} copy-done((bf16[128,128]{1,0:T(8,128)(2,1)S(1)}, bf16[128,128]{1,0:T(8,128)(2,1)}, u32[]{:S(2)}) %copy-start.3) | copy-done | bytes 32792
  9.7 0.3 prepare.1
  10.1 0.0 collective-permute-done.2.three_ref
  10.1 1.8 %collective-permute-done.1.two_ref = bf16[128,128]{1,0:T(8,128)(2,1)S(1)} collective-permute-done((bf16[128,128]{1,0:T(8,128)(2,1)}, bf16[128,128]{1,0:T(8,128)(2,1)S(1)}, u32[]{:S(2)}, u32[]{:S(2)}) %collective-permute-start.1) | collective-permute-done | bytes 32800 | tf_op jit(solution)/shard_map/ppermute | solution.py:369
  11.9 0.3 collective-permute-done.one_ref
  12.2 1.2 %pick.1 = (bf16[512,128]{1,0:T(8,128)(2,1)S(1)}, bf16[32,32,128]{2,1,0:T(8,128)(2,1)}) custom-call(bf16[128,128]{1,0:T(8,128)(2,1)S(1)} %get-tuple-element.15.own_ref, bf16[128,128]{1,0:T(8,128)(2,1)S(1)} %collective-permute-done.one_ref, bf16[128,128]{1,0:T(8,128)(2,1)S(1)} %collective-permute-done.1.two_ref, ...), custom_call_target="tpu_custom_call" | custom-call | flops 134217728 | bytes 1048576 | tf_op jit(solution)/shard_map/pick/pallas_call | solution.py:156
  13.4 10.2 %all-to-all-start = ((bf16[32,32,128]{2,1,0:T(8,128)(2,1)}), bf16[32,32,128]{2,1,0:T(8,128)(2,1)S(1)}, u32[]{:S(2)}, u32[]{:S(2)}) async-start(bf16[32,32,128]{2,1,0:T(8,128)(2,1)} %get-tuple-element.18), calls=%async_computation | async-start | bytes 524288 | tf_op jit(solution)/shard_map/all_to_all | solution.py:376
  23.6 0.0 copy-done.5
  23.6 8.4 %near.1.near_ref = f32[512,128]{1,0:T(8,128)S(1)} custom-call(s16[512,128]{1,0:T(8,128)(2,1)S(1)} %get-tuple-element.14.code_ref, bf16[512,128]{1,0:T(8,128)(2,1)S(1)} %get-tuple-element.17.part_ref, bf16[79,128,128]{2,1,0:T(8,128)(2,1)S(1)} %copy-done.5), custom_call_target="tpu_custom_call" | custom-call | flops 6627000320 | bytes 2588672 | tf_op jit(solution)/shard_map/near/pallas_call | solution.py:240
  32.0 0.3 all-to-all-done.got_ref
  32.3 0.0 copy-start
  32.3 9.4 %far.1 = (f32[128,128]{1,0:T(8,128)S(1)}, bf16[128,128]{1,0:T(8,128)(2,1)S(1)}, bf16[128,128]{1,0:T(8,128)(2,1)S(1)}, bf16[128,128]{1,0:T(8,128)(2,1)S(1)}) custom-call(s16[512,128]{1,0:T(8,128)(2,1)S(1)} %get-tuple-element.14.code_ref, f32[512,128]{1,0:T(8,128)S(1)} %near.1.near_ref, bf16[32,32,128]{2,1,0:T(8,128)(2,1)S(1)} %all-to-all-done.got_ref, ...), custom_call_target="tpu_custom_call" | custom-call | flops 6627000320 | bytes 2588672 | tf_op jit(solution)/shard_map/far/pallas_call | solution.py:293
  41.7 0.1 collective-permute-start.3
  41.8 1.5 %collective-permute-start.4 = (bf16[128,128]{1,0:T(8,128)(2,1)S(1)}, bf16[128,128]{1,0:T(8,128)(2,1)S(1)}, u32[]{:S(2)}, u32[]{:S(2)}) collective-permute-start(bf16[128,128]{1,0:T(8,128)(2,1)S(1)} %get-tuple-element.21), channel_id=1, source_target_pairs={{0,2},{1,3},{2,0},{3,1},{4,6},{5,7},{6,4},{7,5},{8,10},{9,11},{10,... | collective-permute-start | bytes 98312 | tf_op jit(solution)/shard_map/ppermute | solution.py:369
  43.3 0.0 copy-start.1
  43.3 0.0 copy-start.4
  43.3 2.0 %collective-permute-start.5 = (bf16[128,128]{1,0:T(8,128)(2,1)S(1)}, bf16[128,128]{1,0:T(8,128)(2,1)S(1)}, u32[]{:S(2)}, u32[]{:S(2)}) collective-permute-start(bf16[128,128]{1,0:T(8,128)(2,1)S(1)} %get-tuple-element.22), channel_id=1, source_target_pairs={{0,3},{1,0},{2,1},{3,2},{4,7},{5,4},{6,5},{7,6},{8,11},{9,8},{10,9... | collective-permute-start | bytes 98312 | tf_op jit(solution)/shard_map/ppermute | solution.py:369
  45.3 0.0 copy-done
  45.3 1.1 %split.1.l2l_ref = bf16[8,488,488]{2,1,0:T(8,128)(2,1)S(1)} custom-call(bf16[488,8,488]{2,1,0:T(8,128)(2,1)S(1)} %copy-done), custom_call_target="tpu_custom_call" | custom-call | flops 1 | bytes 7620608 | tf_op jit(solution)/shard_map/split/pallas_call | solution.py:184
  46.4 0.0 collective-permute-done.3.one_ref
  46.4 0.0 collective-permute-done.4.two_ref
  46.4 0.6 %collective-permute-done.5.three_ref = bf16[128,128]{1,0:T(8,128)(2,1)S(1)} collective-permute-done((bf16[128,128]{1,0:T(8,128)(2,1)S(1)}, bf16[128,128]{1,0:T(8,128)(2,1)S(1)}, u32[]{:S(2)}, u32[]{:S(2)}) %collective-permute-start.5) | collective-permute-done | bytes 32800 | tf_op jit(solution)/shard_map/ppermute | solution.py:369
  47.0 0.0 copy-done.1
  47.0 0.0 copy-done.4
  47.0 2.3 %downward.1 = bf16[488,1024]{1,0:T(8,128)(2,1)} custom-call(f32[128,128]{1,0:T(8,128)S(1)} %get-tuple-element.19.own_ref, bf16[128,128]{1,0:T(8,128)(2,1)S(1)} %collective-permute-done.3.one_ref, bf16[128,128]{1,0:T(8,128)(2,1)S(1)} %collective-permute-done.4.two_ref, bf16[128,128]{1,0:T(8,128)(2,1)S(1)} %collective-permute-done.5.three_ref, ...), custom_call_target="tpu_custom_call" | custom-call | flops 487718912 | bytes 5809152 | tf_op jit(solution)/shard_map/downward/pallas_call | solution.py:348
Async XLA Ops:
  0.0 8.4 %copy-start.6 = (s32[1,32,32]{2,1,0:T(8,128)S(1)}, s32[1,32,32]{2,1,0:T(8,128)}, u32[]{:S(2)}) copy-start(s32[1,32,32]{2,1,0:T(8,128)} %param.16) | copy-start | bytes 12292
  0.0 9.0 %copy-start.2 = (s32[512,79]{0,1:T(8,128)S(1)}, s32[512,79]{0,1:T(8,128)}, u32[]{:S(2)}) copy-start(s32[512,79]{0,1:T(8,128)} %param.17) | copy-start | bytes 485380
  0.0 23.6 %copy-start.5 = (bf16[79,128,128]{2,1,0:T(8,128)(2,1)S(1)}, bf16[79,128,128]{2,1,0:T(8,128)(2,1)}, u32[]{:S(2)}) copy-start(bf16[79,128,128]{2,1,0:T(8,128)(2,1)} %core_ref.3) | copy-start | bytes 7766020
  3.8 6.3 %collective-permute-start.2 = (bf16[128,128]{1,0:T(8,128)(2,1)}, bf16[128,128]{1,0:T(8,128)(2,1)S(1)}, u32[]{:S(2)}, u32[]{:S(2)}) collective-permute-start(bf16[128,128]{1,0:T(8,128)(2,1)} %upward.1.packed_ref), channel_id=1, source_target_pairs={{0,3},{1,0},{2,1},{3,2},{4,7},{5,4},{6,5},{7,6},{8,11},{9,8},{10,9... | collective-permute-start | bytes 98312 | tf_op jit(solution)/shard_map/ppermute | solution.py:369
  7.4 4.5 %collective-permute-start.1 = (bf16[128,128]{1,0:T(8,128)(2,1)}, bf16[128,128]{1,0:T(8,128)(2,1)S(1)}, u32[]{:S(2)}, u32[]{:S(2)}) collective-permute-start(bf16[128,128]{1,0:T(8,128)(2,1)} %upward.1.packed_ref), channel_id=1, source_target_pairs={{0,2},{1,3},{2,0},{3,1},{4,6},{5,7},{6,4},{7,5},{8,10},{9,11},{10,... | collective-permute-start | bytes 98312 | tf_op jit(solution)/shard_map/ppermute | solution.py:369
  7.7 4.5 %collective-permute-start = (bf16[128,128]{1,0:T(8,128)(2,1)}, bf16[128,128]{1,0:T(8,128)(2,1)S(1)}, u32[]{:S(2)}, u32[]{:S(2)}) collective-permute-start(bf16[128,128]{1,0:T(8,128)(2,1)} %upward.1.packed_ref), channel_id=1, source_target_pairs={{0,1},{1,2},{2,3},{3,0},{4,5},{5,6},{6,7},{7,4},{8,9},{9,10},{10,1... | collective-permute-start | bytes 98312 | tf_op jit(solution)/shard_map/ppermute | solution.py:369
  9.0 0.8 %copy-start.3 = (bf16[128,128]{1,0:T(8,128)(2,1)S(1)}, bf16[128,128]{1,0:T(8,128)(2,1)}, u32[]{:S(2)}) copy-start(bf16[128,128]{1,0:T(8,128)(2,1)} %upward.1.packed_ref) | copy-start | bytes 98308
  13.4 18.9 %all-to-all-start = ((bf16[32,32,128]{2,1,0:T(8,128)(2,1)}), bf16[32,32,128]{2,1,0:T(8,128)(2,1)S(1)}, u32[]{:S(2)}, u32[]{:S(2)}) async-start(bf16[32,32,128]{2,1,0:T(8,128)(2,1)} %get-tuple-element.18), calls=%async_computation | async-start | bytes 524288 | tf_op jit(solution)/shard_map/all_to_all | solution.py:376
  32.3 13.0 %copy-start = (bf16[488,8,488]{2,1,0:T(8,128)(2,1)S(1)}, bf16[488,8,488]{2,1,0:T(8,128)(2,1)}, u32[]{:S(2)}) copy-start(bf16[488,8,488]{2,1,0:T(8,128)(2,1)} %l2l_ref.1) | copy-start | bytes 11430916
  41.7 4.6 %collective-permute-start.3 = (bf16[128,128]{1,0:T(8,128)(2,1)S(1)}, bf16[128,128]{1,0:T(8,128)(2,1)S(1)}, u32[]{:S(2)}, u32[]{:S(2)}) collective-permute-start(bf16[128,128]{1,0:T(8,128)(2,1)S(1)} %get-tuple-element.20), channel_id=1, source_target_pairs={{0,1},{1,2},{2,3},{3,0},{4,5},{5,6},{6,7},{7,4},{8,9},{9,10},{10,1... | collective-permute-start | bytes 98312 | tf_op jit(solution)/shard_map/ppermute | solution.py:369
  41.8 4.6 %collective-permute-start.4 = (bf16[128,128]{1,0:T(8,128)(2,1)S(1)}, bf16[128,128]{1,0:T(8,128)(2,1)S(1)}, u32[]{:S(2)}, u32[]{:S(2)}) collective-permute-start(bf16[128,128]{1,0:T(8,128)(2,1)S(1)} %get-tuple-element.21), channel_id=1, source_target_pairs={{0,2},{1,3},{2,0},{3,1},{4,6},{5,7},{6,4},{7,5},{8,10},{9,11},{10,... | collective-permute-start | bytes 98312 | tf_op jit(solution)/shard_map/ppermute | solution.py:369
  43.3 3.7 %copy-start.1 = (bf16[1024,488]{0,1:T(8,128)(2,1)S(1)}, bf16[1024,488]{0,1:T(8,128)(2,1)}, u32[]{:S(2)}) copy-start(bf16[1024,488]{0,1:T(8,128)(2,1)} %param.15) | copy-start | bytes 2998276
  43.3 3.7 %copy-start.4 = (bf16[128,488]{0,1:T(8,128)(2,1)S(1)}, bf16[128,488]{0,1:T(8,128)(2,1)}, u32[]{:S(2)}) copy-start(bf16[128,488]{0,1:T(8,128)(2,1)} %param.13) | copy-start | bytes 374788
  43.3 3.7 %collective-permute-start.5 = (bf16[128,128]{1,0:T(8,128)(2,1)S(1)}, bf16[128,128]{1,0:T(8,128)(2,1)S(1)}, u32[]{:S(2)}, u32[]{:S(2)}) collective-permute-start(bf16[128,128]{1,0:T(8,128)(2,1)S(1)} %get-tuple-element.22), channel_id=1, source_target_pairs={{0,3},{1,0},{2,1},{3,2},{4,7},{5,4},{6,5},{7,6},{8,11},{9,8},{10,9... | collective-permute-start | bytes 98312 | tf_op jit(solution)/shard_map/ppermute | solution.py:369

commit v4 on v3

--- a/solution.py
+++ b/solution.py
@@ -1,3 +1,5 @@
+import functools
+
 import jax
 import jax.numpy as jnp
 from jax import lax
@@ -24,13 +26,13 @@
     return jnp.dot(a, b, preferred_element_type=F32)
 
 
-def call(kernel, name, out, ins, scratch, limit, flops, nbytes, place=VMEM):
+def call(kernel, name, out, ins, scratch, limit, flops, nbytes):
     return pl.pallas_call(
         kernel,
         name=name,
         out_shape=out,
         in_specs=ins,
-        out_specs=jax.tree.map(lambda _: place, out),
+        out_specs=jax.tree.map(lambda _: VMEM, out),
         scratch_shapes=scratch,
         compiler_params=pltpu.CompilerParams(vmem_limit_bytes=limit * MIB),
         cost_estimate=pl.CostEstimate(flops=flops, bytes_accessed=nbytes, transcendentals=0),
@@ -84,7 +86,7 @@
             pltpu.VMEM(leaf_t.shape, BF),
             pltpu.VMEM(m2m.shape, BF),
             pltpu.VMEM(compress.shape, BF),
-            pltpu.VMEM((-(-width // 128), count * PITCH, 128), F32),
+            pltpu.VMEM((-(-width // 128), (count + 2) * PITCH, 128), F32),
             pltpu.SemaphoreType.DMA((nkids + 2,)),
         ],
         60,
@@ -168,29 +170,31 @@
     )(*pieces, hot)
 
 
-def split_kernel(l2l_ref, out_ref, wide_ref):
+def fold_kernel(expand_ref, l2l_ref, out_ref, wide_ref):
     width, nkids, _ = l2l_ref.shape
+    expand = expand_ref[...].astype(F32).T.astype(BF)
     for i, base in enumerate(range(0, width, 128)):
         size = min(128, width - base)
         block = l2l_ref[:, :, base:base + size].astype(F32)
         for p in range(width):
             wide_ref[i, p * PITCH:p * PITCH + nkids, :size] = block[p]
     for c in range(nkids):
-        out_ref[c] = kid_rows(wide_ref, c, width, width)
-
-
-def split(l2l):
+        out_ref[c] = dot(expand, kid_rows(wide_ref, c, width, width)).astype(BF)
+
+
+def fold(expand_t, l2l):
     width, nkids, _ = l2l.shape
-    return call(
-        split_kernel,
-        "split",
-        jax.ShapeDtypeStruct((nkids, width, width), BF),
-        [VMEM],
-        [pltpu.VMEM((-(-width // 128), width * PITCH, 128), F32)],
+    rank = expand_t.shape[1]
+    return call(
+        fold_kernel,
+        "fold",
+        jax.ShapeDtypeStruct((nkids, rank, width), BF),
+        [VMEM] * 2,
+        [pltpu.VMEM((-(-width // 128), (width + 2) * PITCH, 128), F32)],
         24,
-        1,
-        4 * l2l.size,
-    )(l2l)
+        2 * rank * l2l.size,
+        2 * l2l.size,
+    )(expand_t, l2l)
 
 
 def either(test, both):
@@ -226,8 +230,16 @@
             hots = []
 
 
+def widen(code_ref, wide_ref, shifts):
+    share = code_ref.shape[0] // 4
+    for i, shift in enumerate(shifts):
+        start = lax.rem(lax.axis_index("sub") + shift, 4) * share
+        rows = code_ref[pl.ds(pl.multiple_of(start, share), share), :]
+        wide_ref[i * share:(i + 1) * share, :] = rows.astype(I32)
+
+
 def near_kernel(code_ref, part_ref, core_ref, acc_ref, table_ref, wide_ref):
-    wide_ref[...] = code_ref[...].astype(I32)
+    widen(code_ref, wide_ref, range(4))
     rank = part_ref.shape[1]
     table_ref[:, :rank] = part_ref[:HALF, :]
     table_ref[:, rank:] = part_ref[HALF:, :]
@@ -249,10 +261,10 @@
     )(code, part, core)
 
 
-def far_kernel(code_ref, near_ref, got_ref, core_ref, *rest):
-    outs, (table_ref, wide_ref, acc_ref, z_ref) = rest[:4], rest[4:]
-    wide_ref[...] = code_ref[...].astype(I32)
-    here, me = lax.axis_index("dom"), lax.axis_index("sub")
+def far_kernel(shifts, code_ref, near_ref, got_ref, core_ref, *rest):
+    outs, (table_ref, wide_ref, acc_ref, z_ref) = rest[:len(shifts)], rest[len(shifts):]
+    widen(code_ref, wide_ref, shifts)
+    here = lax.axis_index("dom")
     npart, _, rank = got_ref.shape
     offsets = core_ref.shape[0]
     cut = npart // 2
@@ -277,51 +289,49 @@
         n = min(STEP, offsets - k)
         core = core_ref[k:k + n].reshape(n * rank, rank)
         z_ref[k * SURE:(k + n) * SURE, :] = dot(tail[:n * SURE, :n * rank], core).astype(BF)
-    acc_ref[...] = near_ref[...]
+    share = code_ref.shape[0] // 4
+    for i, shift in enumerate(shifts):
+        acc_ref[i * share:(i + 1) * share, :] = near_ref[shift * share:(shift + 1) * share, :]
     accumulate(wide_ref, 2 * HALF, table_ref, core_ref, acc_ref, z_ref)
-    share = acc_ref.shape[0] // 4
-    for shift, out in enumerate(outs):
-        start = lax.rem(me + shift, 4) * share
-        out[...] = acc_ref[pl.ds(pl.multiple_of(start, share), share), :].astype(out.dtype)
-
-
-def far(code, near_sums, got, core):
-    count, rank = near_sums.shape
+    for i, out in enumerate(outs):
+        out[...] = acc_ref[i * share:(i + 1) * share, :].astype(out.dtype)
+
+
+def far(code, near_sums, got, core, shifts):
+    rank = near_sums.shape[1]
+    share = near_sums.shape[0] // 4
+    count = share * len(shifts)
     offsets = core.shape[0]
     zrows = (offsets * SURE // 128 + 1) * 128
-    piece = (count // 4, rank)
-    return call(
-        far_kernel,
+    return call(
+        functools.partial(far_kernel, shifts),
         "far",
-        tuple(jax.ShapeDtypeStruct(piece, BF if i else F32) for i in range(4)),
+        tuple(jax.ShapeDtypeStruct((share, rank), BF if shift else F32) for shift in shifts),
         [VMEM] * 4,
         [
             pltpu.VMEM((HALF, 2 * rank), BF),
-            pltpu.VMEM(code.shape, I32),
+            pltpu.VMEM((count, 128), I32),
             pltpu.VMEM((count, rank), F32),
             pltpu.VMEM((zrows, rank), BF),
         ],
         24,
-        2 * count * offsets * rank * (count + rank),
+        2 * count * offsets * rank * (4 * share + rank),
         2 * core.size,
     )(code, near_sums, got, core)
 
 
-def down_kernel(own_ref, one_ref, two_ref, three_ref, expand_ref, l2l_ref, inh_ref, out_hbm, rows_ref, out_ref, sems):
-    nkids, width = l2l_ref.shape[0], l2l_ref.shape[1]
+def down_kernel(own_ref, one_ref, two_ref, three_ref, fold_ref, inh_ref, out_ref, rows_ref):
+    nkids, _, width = fold_ref.shape
     count = own_ref.shape[0]
     acc = own_ref[...]
     for ref in (one_ref, two_ref, three_ref):
         acc = acc + ref[...].astype(F32)
-    local = lax.dot_general(
-        acc.astype(BF), expand_ref[...], (((1,), (1,)), ((), ())), preferred_element_type=F32
-    ).astype(BF)
+    acc = acc.astype(BF)
     for c in range(nkids):
-        kid = dot(local, l2l_ref[c])
+        kid = dot(acc, fold_ref[c])
         kid = jnp.concatenate([kid, jnp.zeros((count, -width % 128), F32)], axis=1)
         for i in range(rows_ref.shape[0]):
             rows_ref[i, pl.ds(c, count, stride=PITCH), :] = kid[:, i * 128:(i + 1) * 128]
-    copies = []
     for i, base in enumerate(range(0, width, 128)):
         rows = slice(base, min(base + 128, width))
         for j in range(out_ref.shape[1] // 128):
@@ -335,31 +345,21 @@
                 axis=0,
             ).T[:rows.stop - base]
             out_ref[rows, cols] = (far + inh_ref[rows, cols].astype(F32)).astype(BF)
-        part = pl.ds(base, rows.stop - base)
-        copies.append(pltpu.make_async_copy(out_ref.at[part], out_hbm.at[part], sems.at[i]))
-        copies[-1].start()
-    for copy in copies:
-        copy.wait()
-
-
-def downward(pieces, expand_t, l2l, inherited_t):
-    nkids, width, _ = l2l.shape
+
+
+def downward(pieces, folded, inherited_t):
+    nkids, rank, width = folded.shape
     blocks = -(-width // 128)
     return call(
         down_kernel,
         "downward",
         jax.ShapeDtypeStruct(inherited_t.shape, BF),
-        [VMEM] * 7,
-        [
-            pltpu.VMEM((blocks, pieces[0].shape[0] * PITCH, 128), F32),
-            pltpu.VMEM(inherited_t.shape, BF),
-            pltpu.SemaphoreType.DMA((blocks,)),
-        ],
+        [VMEM] * 6,
+        [pltpu.VMEM((blocks, (pieces[0].shape[0] + 2) * PITCH, 128), F32)],
         32,
-        2 * inherited_t.size * width,
-        2 * (2 * inherited_t.size + l2l.size),
-        HBM,
-    )(*pieces, expand_t, l2l, inherited_t)
+        2 * inherited_t.size * rank,
+        2 * (2 * inherited_t.size + folded.size),
+    )(*pieces, folded, inherited_t)
 
 
 def local(leaf_mult, m2m, compress, m2l_core, expand, l2l, inherited, send_rows, m2l_list):
@@ -371,13 +371,13 @@
     packed = upward(leaf_mult.T, m2m, compress)
     moved = [shifted(packed, shift) for shift in (1, 2, 3)]
     code, hot, own = prepare(m2l_list.T, send_rows.reshape(npart * CAP, 1), packed)
-    kids = split(l2l)
+    folded = fold(expand.T, l2l)
     part, send = pick([own] + moved, hot, npart)
     got = lax.all_to_all(send, "dom", 0, 0, tiled=True)
     near_sums = near(code, part, m2l_core)
-    sums = far(code, near_sums, got, m2l_core)
+    sums = far(code, near_sums, got, m2l_core, (0, 1, 2, 3))
     sums = [sums[0]] + [shifted(sums[shift], shift) for shift in (1, 2, 3)]
-    return downward(sums, expand.T, kids, inherited.T).T
+    return downward(sums, folded, inherited.T).T
 
 
 def solution(mesh):

time: 49.7 us -> 49.2 us (0.990)
  transfers between devices with their start and end apart: 7 -> 7, of which waited for: 4 -> 4; matrix products, arithmetic and copies ran while one was open for 1% -> 1% of each run, Pallas kernels for 20% -> 21%
where the time goes in v4:
time: 49.2 us; the launch traced here: 48.9 us
  Pallas kernels  26.4 us (54%)
  starting transfers between devices  18.4 us (37%)
  waiting for transfers between devices  2.7 us (5%)
  local copies, waits for them, and re-layouts  1.31 us (3%)
    all_to_all x1, starting transfers between devices, local(): got = lax.all_to_all(send, 'dom', 0, 0, tiled=True)  10.2 us
    pallas_call x1, Pallas kernels, far(): call(functools.partial(far_kernel, shifts), 'far', tuple((jax.ShapeDtypeS...  9.39 us
    pallas_call x1, Pallas kernels, near(): call(near_kernel, 'near', jax.ShapeDtypeStruct((count, rank), F32), [VMEM...  8.41 us
    ppermute x6, starting transfers between devices, shifted(): lax.ppermute(x, 'sub', [(i, (i + shift) % nsub) for i in range(nsub)])  8.21 us
    pallas_call x1, Pallas kernels, upward(): call(up_kernel, 'upward', jax.ShapeDtypeStruct((count, compress.shape[1])...  3.73 us
    ppermute x6, waiting for transfers between devices, shifted(): lax.ppermute(x, 'sub', [(i, (i + shift) % nsub) for i in range(nsub)])  2.41 us
    pallas_call x1, Pallas kernels, downward(): call(down_kernel, 'downward', jax.ShapeDtypeStruct(inherited_t.shape, BF)...  1.95 us
    pallas_call x1, Pallas kernels, fold(): call(fold_kernel, 'fold', jax.ShapeDtypeStruct((nkids, rank, width), BF),...  1.4 us
  transfers between devices with their start and end apart: 7, of which 4 were waited for; matrix products, arithmetic and copies ran while one was open for 1% of the time, Pallas kernels for 21%

profile of v4, /device:TPU:1, one launch (start us, length us, event | category | flops | bytes accessed | tf_op | source)
XLA Modules:
  0.0 48.9 jit_solution(2960210669410946745)
XLA Ops:
  0.0 0.0 copy-start.6
  0.0 0.0 copy-start.2
  0.0 0.0 copy-start.5
  0.0 3.7 %upward.1.packed_ref = bf16[128,128]{1,0:T(8,128)(2,1)} custom-call(bf16[488,1024]{1,0:T(8,128)(2,1)} %bitcast.8, bf16[8,488,488]{2,1,0:T(8,128)(2,1)} %m2m_ref.1, bf16[488,128]{1,0:T(8,128)(2,1)} %compress_ref.1), custom_call_target="tpu_custom_call" | custom-call | flops 487718912 | bytes 4809728 | tf_op jit(solution)/shard_map/upward/pallas_call | solution.py:80
  3.7 3.6 %collective-permute-start.2 = (bf16[128,128]{1,0:T(8,128)(2,1)}, bf16[128,128]{1,0:T(8,128)(2,1)S(1)}, u32[]{:S(2)}, u32[]{:S(2)}) collective-permute-start(bf16[128,128]{1,0:T(8,128)(2,1)} %upward.1.packed_ref), channel_id=1, source_target_pairs={{0,3},{1,0},{2,1},{3,2},{4,7},{5,4},{6,5},{7,6},{8,11},{9,8},{10,9... | collective-permute-start | bytes 98312 | tf_op jit(solution)/shard_map/ppermute | solution.py:369
  7.4 0.4 collective-permute-start.1
  7.7 0.7 %collective-permute-start = (bf16[128,128]{1,0:T(8,128)(2,1)}, bf16[128,128]{1,0:T(8,128)(2,1)S(1)}, u32[]{:S(2)}, u32[]{:S(2)}) collective-permute-start(bf16[128,128]{1,0:T(8,128)(2,1)} %upward.1.packed_ref), channel_id=1, source_target_pairs={{0,1},{1,2},{2,3},{3,0},{4,5},{5,6},{6,7},{7,4},{8,9},{9,10},{10,1... | collective-permute-start | bytes 98312 | tf_op jit(solution)/shard_map/ppermute | solution.py:369
  8.4 0.0 copy-done.6
  8.4 0.5 %reshape.4.rows_ref = s32[1024,1]{1,0:T(8,128)S(1)} reshape(s32[1,32,32]{2,1,0:T(8,128)S(1)} %copy-done.6) | data formatting | bytes 8192 | tf_op jit(solution)/shard_map/reshape | solution.py:373
  9.0 0.0 copy-done.2
  9.0 0.0 copy-start.3
  9.0 0.7 %copy-done.3 = bf16[128,128]{1,0:T(8,128)(2,1)S(1)} copy-done((bf16[128,128]{1,0:T(8,128)(2,1)S(1)}, bf16[128,128]{1,0:T(8,128)(2,1)}, u32[]{:S(2)}) %copy-start.3) | copy-done | bytes 32792
  9.7 0.3 prepare.1
  10.1 0.0 collective-permute-done.2.three_ref
  10.1 1.8 %collective-permute-done.1.two_ref = bf16[128,128]{1,0:T(8,128)(2,1)S(1)} collective-permute-done((bf16[128,128]{1,0:T(8,128)(2,1)}, bf16[128,128]{1,0:T(8,128)(2,1)S(1)}, u32[]{:S(2)}, u32[]{:S(2)}) %collective-permute-start.1) | collective-permute-done | bytes 32800 | tf_op jit(solution)/shard_map/ppermute | solution.py:369
  11.9 0.3 collective-permute-done.one_ref
  12.2 1.2 %pick.1 = (bf16[512,128]{1,0:T(8,128)(2,1)S(1)}, bf16[32,32,128]{2,1,0:T(8,128)(2,1)}) custom-call(bf16[128,128]{1,0:T(8,128)(2,1)S(1)} %get-tuple-element.15.own_ref, bf16[128,128]{1,0:T(8,128)(2,1)S(1)} %collective-permute-done.one_ref, bf16[128,128]{1,0:T(8,128)(2,1)S(1)} %collective-permute-done.1.two_ref, ...), custom_call_target="tpu_custom_call" | custom-call | flops 134217728 | bytes 1048576 | tf_op jit(solution)/shard_map/pick/pallas_call | solution.py:158
  13.4 10.2 %all-to-all-start = ((bf16[32,32,128]{2,1,0:T(8,128)(2,1)}), bf16[32,32,128]{2,1,0:T(8,128)(2,1)S(1)}, u32[]{:S(2)}, u32[]{:S(2)}) async-start(bf16[32,32,128]{2,1,0:T(8,128)(2,1)} %get-tuple-element.18), calls=%async_computation | async-start | bytes 524288 | tf_op jit(solution)/shard_map/all_to_all | solution.py:376
  23.6 0.0 copy-done.5
  23.6 8.4 %near.1.near_ref = f32[512,128]{1,0:T(8,128)S(1)} custom-call(s16[512,128]{1,0:T(8,128)(2,1)S(1)} %get-tuple-element.14.code_ref, bf16[512,128]{1,0:T(8,128)(2,1)S(1)} %get-tuple-element.17.part_ref, bf16[79,128,128]{2,1,0:T(8,128)(2,1)S(1)} %copy-done.5), custom_call_target="tpu_custom_call" | custom-call | flops 6627000320 | bytes 2588672 | tf_op jit(solution)/shard_map/near/pallas_call | solution.py:252
  32.0 0.0 copy-start.4
  32.0 0.3 all-to-all-done.got_ref
  32.3 0.0 copy-start
  32.3 9.4 %far.1 = (f32[128,128]{1,0:T(8,128)S(1)}, bf16[128,128]{1,0:T(8,128)(2,1)S(1)}, bf16[128,128]{1,0:T(8,128)(2,1)S(1)}, bf16[128,128]{1,0:T(8,128)(2,1)S(1)}) custom-call(s16[512,128]{1,0:T(8,128)(2,1)S(1)} %get-tuple-element.14.code_ref, f32[512,128]{1,0:T(8,128)S(1)} %near.1.near_ref, bf16[32,32,128]{2,1,0:T(8,128)(2,1)S(1)} %all-to-all-done.got_ref, ...), custom_call_target="tpu_custom_call" | custom-call | flops 6627000320 | bytes 2588672 | tf_op jit(solution)/shard_map/far/pallas_call | solution.py:306
  41.7 0.0 copy-start.1
  41.7 0.1 collective-permute-start.3
  41.8 1.5 %collective-permute-start.4 = (bf16[128,128]{1,0:T(8,128)(2,1)S(1)}, bf16[128,128]{1,0:T(8,128)(2,1)S(1)}, u32[]{:S(2)}, u32[]{:S(2)}) collective-permute-start(bf16[128,128]{1,0:T(8,128)(2,1)S(1)} %get-tuple-element.21), channel_id=1, source_target_pairs={{0,2},{1,3},{2,0},{3,1},{4,6},{5,7},{6,4},{7,5},{8,10},{9,11},{10,... | collective-permute-start | bytes 98312 | tf_op jit(solution)/shard_map/ppermute | solution.py:369
  43.3 2.0 %collective-permute-start.5 = (bf16[128,128]{1,0:T(8,128)(2,1)S(1)}, bf16[128,128]{1,0:T(8,128)(2,1)S(1)}, u32[]{:S(2)}, u32[]{:S(2)}) collective-permute-start(bf16[128,128]{1,0:T(8,128)(2,1)S(1)} %get-tuple-element.22), channel_id=1, source_target_pairs={{0,3},{1,0},{2,1},{3,2},{4,7},{5,4},{6,5},{7,6},{8,11},{9,8},{10,9... | collective-permute-start | bytes 98312 | tf_op jit(solution)/shard_map/ppermute | solution.py:369
  45.3 0.0 copy-done.4
  45.3 0.0 copy-done
  45.3 1.4 %fold.1.fold_ref = bf16[8,128,488]{2,1,0:T(8,128)(2,1)S(1)} custom-call(bf16[488,128]{1,0:T(8,128)(2,1)S(1)} %bitcast.7, bf16[488,8,488]{2,1,0:T(8,128)(2,1)S(1)} %copy-done), custom_call_target="tpu_custom_call" | custom-call | flops 487718912 | bytes 3810304 | tf_op jit(solution)/shard_map/fold/pallas_call | solution.py:188
  46.7 0.0 collective-permute-done.3.one_ref
  46.7 0.0 collective-permute-done.4.two_ref
  46.7 0.3 collective-permute-done.5.three_ref
  47.0 0.0 copy-done.1
  47.0 2.0 %downward.1 = bf16[488,1024]{1,0:T(8,128)(2,1)} custom-call(f32[128,128]{1,0:T(8,128)S(1)} %get-tuple-element.19.own_ref, bf16[128,128]{1,0:T(8,128)(2,1)S(1)} %collective-permute-done.3.one_ref, bf16[128,128]{1,0:T(8,128)(2,1)S(1)} %collective-permute-done.4.two_ref, bf16[128,128]{1,0:T(8,128)(2,1)S(1)} %collective-permute-done.5.three_ref, ...), custom_call_target="tpu_custom_call" | custom-call | flops 127926272 | bytes 2998272 | tf_op jit(solution)/shard_map/downward/pallas_call | solution.py:353
Async XLA Ops:
  0.0 8.4 %copy-start.6 = (s32[1,32,32]{2,1,0:T(8,128)S(1)}, s32[1,32,32]{2,1,0:T(8,128)}, u32[]{:S(2)}) copy-start(s32[1,32,32]{2,1,0:T(8,128)} %param.16) | copy-start | bytes 12292
  0.0 9.0 %copy-start.2 = (s32[512,79]{0,1:T(8,128)S(1)}, s32[512,79]{0,1:T(8,128)}, u32[]{:S(2)}) copy-start(s32[512,79]{0,1:T(8,128)} %param.17) | copy-start | bytes 485380
  0.0 23.6 %copy-start.5 = (bf16[79,128,128]{2,1,0:T(8,128)(2,1)S(1)}, bf16[79,128,128]{2,1,0:T(8,128)(2,1)}, u32[]{:S(2)}) copy-start(bf16[79,128,128]{2,1,0:T(8,128)(2,1)} %core_ref.3) | copy-start | bytes 7766020
  3.7 6.4 %collective-permute-start.2 = (bf16[128,128]{1,0:T(8,128)(2,1)}, bf16[128,128]{1,0:T(8,128)(2,1)S(1)}, u32[]{:S(2)}, u32[]{:S(2)}) collective-permute-start(bf16[128,128]{1,0:T(8,128)(2,1)} %upward.1.packed_ref), channel_id=1, source_target_pairs={{0,3},{1,0},{2,1},{3,2},{4,7},{5,4},{6,5},{7,6},{8,11},{9,8},{10,9... | collective-permute-start | bytes 98312 | tf_op jit(solution)/shard_map/ppermute | solution.py:369
  7.4 4.5 %collective-permute-start.1 = (bf16[128,128]{1,0:T(8,128)(2,1)}, bf16[128,128]{1,0:T(8,128)(2,1)S(1)}, u32[]{:S(2)}, u32[]{:S(2)}) collective-permute-start(bf16[128,128]{1,0:T(8,128)(2,1)} %upward.1.packed_ref), channel_id=1, source_target_pairs={{0,2},{1,3},{2,0},{3,1},{4,6},{5,7},{6,4},{7,5},{8,10},{9,11},{10,... | collective-permute-start | bytes 98312 | tf_op jit(solution)/shard_map/ppermute | solution.py:369
  7.7 4.5 %collective-permute-start = (bf16[128,128]{1,0:T(8,128)(2,1)}, bf16[128,128]{1,0:T(8,128)(2,1)S(1)}, u32[]{:S(2)}, u32[]{:S(2)}) collective-permute-start(bf16[128,128]{1,0:T(8,128)(2,1)} %upward.1.packed_ref), channel_id=1, source_target_pairs={{0,1},{1,2},{2,3},{3,0},{4,5},{5,6},{6,7},{7,4},{8,9},{9,10},{10,1... | collective-permute-start | bytes 98312 | tf_op jit(solution)/shard_map/ppermute | solution.py:369
  9.0 0.8 %copy-start.3 = (bf16[128,128]{1,0:T(8,128)(2,1)S(1)}, bf16[128,128]{1,0:T(8,128)(2,1)}, u32[]{:S(2)}) copy-start(bf16[128,128]{1,0:T(8,128)(2,1)} %upward.1.packed_ref) | copy-start | bytes 98308
  13.4 18.9 %all-to-all-start = ((bf16[32,32,128]{2,1,0:T(8,128)(2,1)}), bf16[32,32,128]{2,1,0:T(8,128)(2,1)S(1)}, u32[]{:S(2)}, u32[]{:S(2)}) async-start(bf16[32,32,128]{2,1,0:T(8,128)(2,1)} %get-tuple-element.18), calls=%async_computation | async-start | bytes 524288 | tf_op jit(solution)/shard_map/all_to_all | solution.py:376
  32.0 13.3 %copy-start.4 = (bf16[128,488]{0,1:T(8,128)(2,1)S(1)}, bf16[128,488]{0,1:T(8,128)(2,1)}, u32[]{:S(2)}) copy-start(bf16[128,488]{0,1:T(8,128)(2,1)} %param.13) | copy-start | bytes 374788
  32.3 13.0 %copy-start = (bf16[488,8,488]{2,1,0:T(8,128)(2,1)S(1)}, bf16[488,8,488]{2,1,0:T(8,128)(2,1)}, u32[]{:S(2)}) copy-start(bf16[488,8,488]{2,1,0:T(8,128)(2,1)} %l2l_ref.1) | copy-start | bytes 11430916
  41.7 5.3 %copy-start.1 = (bf16[1024,488]{0,1:T(8,128)(2,1)S(1)}, bf16[1024,488]{0,1:T(8,128)(2,1)}, u32[]{:S(2)}) copy-start(bf16[1024,488]{0,1:T(8,128)(2,1)} %param.15) | copy-start | bytes 2998276
  41.7 5.0 %collective-permute-start.3 = (bf16[128,128]{1,0:T(8,128)(2,1)S(1)}, bf16[128,128]{1,0:T(8,128)(2,1)S(1)}, u32[]{:S(2)}, u32[]{:S(2)}) collective-permute-start(bf16[128,128]{1,0:T(8,128)(2,1)S(1)} %get-tuple-element.20), channel_id=1, source_target_pairs={{0,1},{1,2},{2,3},{3,0},{4,5},{5,6},{6,7},{7,4},{8,9},{9,10},{10,1... | collective-permute-start | bytes 98312 | tf_op jit(solution)/shard_map/ppermute | solution.py:369
  41.8 4.9 %collective-permute-start.4 = (bf16[128,128]{1,0:T(8,128)(2,1)S(1)}, bf16[128,128]{1,0:T(8,128)(2,1)S(1)}, u32[]{:S(2)}, u32[]{:S(2)}) collective-permute-start(bf16[128,128]{1,0:T(8,128)(2,1)S(1)} %get-tuple-element.21), channel_id=1, source_target_pairs={{0,2},{1,3},{2,0},{3,1},{4,6},{5,7},{6,4},{7,5},{8,10},{9,11},{10,... | collective-permute-start | bytes 98312 | tf_op jit(solution)/shard_map/ppermute | solution.py:369
  43.3 3.7 %collective-permute-start.5 = (bf16[128,128]{1,0:T(8,128)(2,1)S(1)}, bf16[128,128]{1,0:T(8,128)(2,1)S(1)}, u32[]{:S(2)}, u32[]{:S(2)}) collective-permute-start(bf16[128,128]{1,0:T(8,128)(2,1)S(1)} %get-tuple-element.22), channel_id=1, source_target_pairs={{0,3},{1,0},{2,1},{3,2},{4,7},{5,4},{6,5},{7,6},{8,11},{9,8},{10,9... | collective-permute-start | bytes 98312 | tf_op jit(solution)/shard_map/ppermute | solution.py:369

commit v5 on v4

--- a/solution.py
+++ b/solution.py
@@ -375,8 +375,9 @@
     part, send = pick([own] + moved, hot, npart)
     got = lax.all_to_all(send, "dom", 0, 0, tiled=True)
     near_sums = near(code, part, m2l_core)
-    sums = far(code, near_sums, got, m2l_core, (0, 1, 2, 3))
-    sums = [sums[0]] + [shifted(sums[shift], shift) for shift in (1, 2, 3)]
+    order = (0, 2, 1, 3)
+    sums = far(code, near_sums, got, m2l_core, order)
+    sums = [shifted(x, shift) if shift else x for x, shift in zip(sums, order)]
     return downward(sums, folded, inherited.T).T
 
 

time: 49.2 us -> 49.8 us (1.012)
  starting transfers between devices: 18.4 us -> 19 us
    ppermute x6, starting transfers between devices: 8.21 us -> 8.83 us  [shifted(): lax.ppermute(x, 'sub', [(i, (i + shift) % nsub) for i in range(nsub)])]
  transfers between devices with their start and end apart: 7 -> 7, of which waited for: 4 -> 3; matrix products, arithmetic and copies ran while one was open for 1% -> 1% of each run, Pallas kernels for 21% -> 21%
where the time goes in v5:
time: 49.8 us; the launch traced here: 49.3 us
  Pallas kernels  26.4 us (53%)
  starting transfers between devices  19 us (38%)
  waiting for transfers between devices  2.41 us (5%)
  local copies, waits for them, and re-layouts  1.31 us (3%)
    all_to_all x1, starting transfers between devices, local(): got = lax.all_to_all(send, 'dom', 0, 0, tiled=True)  10.2 us
    pallas_call x1, Pallas kernels, far(): call(functools.partial(far_kernel, shifts), 'far', tuple((jax.ShapeDtypeS...  9.39 us
    ppermute x6, starting transfers between devices, shifted(): lax.ppermute(x, 'sub', [(i, (i + shift) % nsub) for i in range(nsub)])  8.83 us
    pallas_call x1, Pallas kernels, near(): call(near_kernel, 'near', jax.ShapeDtypeStruct((count, rank), F32), [VMEM...  8.41 us
    pallas_call x1, Pallas kernels, upward(): call(up_kernel, 'upward', jax.ShapeDtypeStruct((count, compress.shape[1])...  3.73 us
    ppermute x6, waiting for transfers between devices, shifted(): lax.ppermute(x, 'sub', [(i, (i + shift) % nsub) for i in range(nsub)])  2.12 us
    pallas_call x1, Pallas kernels, downward(): call(down_kernel, 'downward', jax.ShapeDtypeStruct(inherited_t.shape, BF)...  1.95 us
    pallas_call x1, Pallas kernels, fold(): call(fold_kernel, 'fold', jax.ShapeDtypeStruct((nkids, rank, width), BF),...  1.4 us
  transfers between devices with their start and end apart: 7, of which 3 were waited for; matrix products, arithmetic and copies ran while one was open for 1% of the time, Pallas kernels for 21%

profile of v5, /device:TPU:1, one launch (start us, length us, event | category | flops | bytes accessed | tf_op | source)
XLA Modules:
  0.0 49.3 jit_solution(9129875893699209145)
XLA Ops:
  0.0 0.0 copy-start.6
  0.0 0.0 copy-start.2
  0.0 0.0 copy-start.5
  0.0 3.7 %upward.1.packed_ref = bf16[128,128]{1,0:T(8,128)(2,1)} custom-call(bf16[488,1024]{1,0:T(8,128)(2,1)} %bitcast.8, bf16[8,488,488]{2,1,0:T(8,128)(2,1)} %m2m_ref.1, bf16[488,128]{1,0:T(8,128)(2,1)} %compress_ref.1), custom_call_target="tpu_custom_call" | custom-call | flops 487718912 | bytes 4809728 | tf_op jit(solution)/shard_map/upward/pallas_call | solution.py:80
  3.7 3.6 %collective-permute-start.2 = (bf16[128,128]{1,0:T(8,128)(2,1)}, bf16[128,128]{1,0:T(8,128)(2,1)S(1)}, u32[]{:S(2)}, u32[]{:S(2)}) collective-permute-start(bf16[128,128]{1,0:T(8,128)(2,1)} %upward.1.packed_ref), channel_id=1, source_target_pairs={{0,3},{1,0},{2,1},{3,2},{4,7},{5,4},{6,5},{7,6},{8,11},{9,8},{10,9... | collective-permute-start | bytes 98312 | tf_op jit(solution)/shard_map/ppermute | solution.py:369
  7.4 0.4 collective-permute-start.1
  7.7 0.7 %collective-permute-start = (bf16[128,128]{1,0:T(8,128)(2,1)}, bf16[128,128]{1,0:T(8,128)(2,1)S(1)}, u32[]{:S(2)}, u32[]{:S(2)}) collective-permute-start(bf16[128,128]{1,0:T(8,128)(2,1)} %upward.1.packed_ref), channel_id=1, source_target_pairs={{0,1},{1,2},{2,3},{3,0},{4,5},{5,6},{6,7},{7,4},{8,9},{9,10},{10,1... | collective-permute-start | bytes 98312 | tf_op jit(solution)/shard_map/ppermute | solution.py:369
  8.4 0.0 copy-done.6
  8.4 0.5 %reshape.4.rows_ref = s32[1024,1]{1,0:T(8,128)S(1)} reshape(s32[1,32,32]{2,1,0:T(8,128)S(1)} %copy-done.6) | data formatting | bytes 8192 | tf_op jit(solution)/shard_map/reshape | solution.py:373
  9.0 0.0 copy-done.2
  9.0 0.0 copy-start.3
  9.0 0.7 %copy-done.3 = bf16[128,128]{1,0:T(8,128)(2,1)S(1)} copy-done((bf16[128,128]{1,0:T(8,128)(2,1)S(1)}, bf16[128,128]{1,0:T(8,128)(2,1)}, u32[]{:S(2)}) %copy-start.3) | copy-done | bytes 32792
  9.7 0.3 prepare.1
  10.1 0.0 collective-permute-done.2.three_ref
  10.1 1.8 %collective-permute-done.1.two_ref = bf16[128,128]{1,0:T(8,128)(2,1)S(1)} collective-permute-done((bf16[128,128]{1,0:T(8,128)(2,1)}, bf16[128,128]{1,0:T(8,128)(2,1)S(1)}, u32[]{:S(2)}, u32[]{:S(2)}) %collective-permute-start.1) | collective-permute-done | bytes 32800 | tf_op jit(solution)/shard_map/ppermute | solution.py:369
  11.9 0.3 collective-permute-done.one_ref
  12.2 1.2 %pick.1 = (bf16[512,128]{1,0:T(8,128)(2,1)S(1)}, bf16[32,32,128]{2,1,0:T(8,128)(2,1)}) custom-call(bf16[128,128]{1,0:T(8,128)(2,1)S(1)} %get-tuple-element.15.own_ref, bf16[128,128]{1,0:T(8,128)(2,1)S(1)} %collective-permute-done.one_ref, bf16[128,128]{1,0:T(8,128)(2,1)S(1)} %collective-permute-done.1.two_ref, ...), custom_call_target="tpu_custom_call" | custom-call | flops 134217728 | bytes 1048576 | tf_op jit(solution)/shard_map/pick/pallas_call | solution.py:158
  13.4 10.2 %all-to-all-start = ((bf16[32,32,128]{2,1,0:T(8,128)(2,1)}), bf16[32,32,128]{2,1,0:T(8,128)(2,1)S(1)}, u32[]{:S(2)}, u32[]{:S(2)}) async-start(bf16[32,32,128]{2,1,0:T(8,128)(2,1)} %get-tuple-element.18), calls=%async_computation | async-start | bytes 524288 | tf_op jit(solution)/shard_map/all_to_all | solution.py:376
  23.6 0.0 copy-done.5
  23.6 8.4 %near.1.near_ref = f32[512,128]{1,0:T(8,128)S(1)} custom-call(s16[512,128]{1,0:T(8,128)(2,1)S(1)} %get-tuple-element.14.code_ref, bf16[512,128]{1,0:T(8,128)(2,1)S(1)} %get-tuple-element.17.part_ref, bf16[79,128,128]{2,1,0:T(8,128)(2,1)S(1)} %copy-done.5), custom_call_target="tpu_custom_call" | custom-call | flops 6627000320 | bytes 2588672 | tf_op jit(solution)/shard_map/near/pallas_call | solution.py:252
  32.0 0.0 copy-start.4
  32.0 0.3 all-to-all-done.got_ref
  32.3 0.0 copy-start
  32.3 9.4 %far.1 = (f32[128,128]{1,0:T(8,128)S(1)}, bf16[128,128]{1,0:T(8,128)(2,1)S(1)}, bf16[128,128]{1,0:T(8,128)(2,1)S(1)}, bf16[128,128]{1,0:T(8,128)(2,1)S(1)}) custom-call(s16[512,128]{1,0:T(8,128)(2,1)S(1)} %get-tuple-element.14.code_ref, f32[512,128]{1,0:T(8,128)S(1)} %near.1.near_ref, bf16[32,32,128]{2,1,0:T(8,128)(2,1)S(1)} %all-to-all-done.got_ref, ...), custom_call_target="tpu_custom_call" | custom-call | flops 6627000320 | bytes 2588672 | tf_op jit(solution)/shard_map/far/pallas_call | solution.py:306
  41.7 0.0 copy-start.1
  41.7 1.5 %collective-permute-start.3 = (bf16[128,128]{1,0:T(8,128)(2,1)S(1)}, bf16[128,128]{1,0:T(8,128)(2,1)S(1)}, u32[]{:S(2)}, u32[]{:S(2)}) collective-permute-start(bf16[128,128]{1,0:T(8,128)(2,1)S(1)} %get-tuple-element.20), channel_id=1, source_target_pairs={{0,2},{1,3},{2,0},{3,1},{4,6},{5,7},{6,4},{7,5},{8,10},{9,11},{10,... | collective-permute-start | bytes 98312 | tf_op jit(solution)/shard_map/ppermute | solution.py:369
  43.2 0.0 collective-permute-start.4
  43.2 2.7 %collective-permute-start.5 = (bf16[128,128]{1,0:T(8,128)(2,1)S(1)}, bf16[128,128]{1,0:T(8,128)(2,1)S(1)}, u32[]{:S(2)}, u32[]{:S(2)}) collective-permute-start(bf16[128,128]{1,0:T(8,128)(2,1)S(1)} %get-tuple-element.22), channel_id=1, source_target_pairs={{0,3},{1,0},{2,1},{3,2},{4,7},{5,4},{6,5},{7,6},{8,11},{9,8},{10,9... | collective-permute-start | bytes 98312 | tf_op jit(solution)/shard_map/ppermute | solution.py:369
  45.9 0.0 copy-done.4
  45.9 0.0 copy-done
  45.9 1.4 %fold.1.fold_ref = bf16[8,128,488]{2,1,0:T(8,128)(2,1)S(1)} custom-call(bf16[488,128]{1,0:T(8,128)(2,1)S(1)} %bitcast.7, bf16[488,8,488]{2,1,0:T(8,128)(2,1)S(1)} %copy-done), custom_call_target="tpu_custom_call" | custom-call | flops 487718912 | bytes 3810304 | tf_op jit(solution)/shard_map/fold/pallas_call | solution.py:188
  47.3 0.0 collective-permute-done.3.one_ref
  47.3 0.0 collective-permute-done.4.two_ref
  47.3 0.0 collective-permute-done.5.three_ref
  47.3 0.0 copy-done.1
  47.3 2.0 %downward.1 = bf16[488,1024]{1,0:T(8,128)(2,1)} custom-call(f32[128,128]{1,0:T(8,128)S(1)} %get-tuple-element.19.own_ref, bf16[128,128]{1,0:T(8,128)(2,1)S(1)} %collective-permute-done.3.one_ref, bf16[128,128]{1,0:T(8,128)(2,1)S(1)} %collective-permute-done.4.two_ref, bf16[128,128]{1,0:T(8,128)(2,1)S(1)} %collective-permute-done.5.three_ref, ...), custom_call_target="tpu_custom_call" | custom-call | flops 127926272 | bytes 2998272 | tf_op jit(solution)/shard_map/downward/pallas_call | solution.py:353
Async XLA Ops:
  0.0 8.4 %copy-start.6 = (s32[1,32,32]{2,1,0:T(8,128)S(1)}, s32[1,32,32]{2,1,0:T(8,128)}, u32[]{:S(2)}) copy-start(s32[1,32,32]{2,1,0:T(8,128)} %param.16) | copy-start | bytes 12292
  0.0 9.0 %copy-start.2 = (s32[512,79]{0,1:T(8,128)S(1)}, s32[512,79]{0,1:T(8,128)}, u32[]{:S(2)}) copy-start(s32[512,79]{0,1:T(8,128)} %param.17) | copy-start | bytes 485380
  0.0 23.6 %copy-start.5 = (bf16[79,128,128]{2,1,0:T(8,128)(2,1)S(1)}, bf16[79,128,128]{2,1,0:T(8,128)(2,1)}, u32[]{:S(2)}) copy-start(bf16[79,128,128]{2,1,0:T(8,128)(2,1)} %core_ref.3) | copy-start | bytes 7766020
  3.7 6.4 %collective-permute-start.2 = (bf16[128,128]{1,0:T(8,128)(2,1)}, bf16[128,128]{1,0:T(8,128)(2,1)S(1)}, u32[]{:S(2)}, u32[]{:S(2)}) collective-permute-start(bf16[128,128]{1,0:T(8,128)(2,1)} %upward.1.packed_ref), channel_id=1, source_target_pairs={{0,3},{1,0},{2,1},{3,2},{4,7},{5,4},{6,5},{7,6},{8,11},{9,8},{10,9... | collective-permute-start | bytes 98312 | tf_op jit(solution)/shard_map/ppermute | solution.py:369
  7.4 4.5 %collective-permute-start.1 = (bf16[128,128]{1,0:T(8,128)(2,1)}, bf16[128,128]{1,0:T(8,128)(2,1)S(1)}, u32[]{:S(2)}, u32[]{:S(2)}) collective-permute-start(bf16[128,128]{1,0:T(8,128)(2,1)} %upward.1.packed_ref), channel_id=1, source_target_pairs={{0,2},{1,3},{2,0},{3,1},{4,6},{5,7},{6,4},{7,5},{8,10},{9,11},{10,... | collective-permute-start | bytes 98312 | tf_op jit(solution)/shard_map/ppermute | solution.py:369
  7.7 4.5 %collective-permute-start = (bf16[128,128]{1,0:T(8,128)(2,1)}, bf16[128,128]{1,0:T(8,128)(2,1)S(1)}, u32[]{:S(2)}, u32[]{:S(2)}) collective-permute-start(bf16[128,128]{1,0:T(8,128)(2,1)} %upward.1.packed_ref), channel_id=1, source_target_pairs={{0,1},{1,2},{2,3},{3,0},{4,5},{5,6},{6,7},{7,4},{8,9},{9,10},{10,1... | collective-permute-start | bytes 98312 | tf_op jit(solution)/shard_map/ppermute | solution.py:369
  9.0 0.8 %copy-start.3 = (bf16[128,128]{1,0:T(8,128)(2,1)S(1)}, bf16[128,128]{1,0:T(8,128)(2,1)}, u32[]{:S(2)}) copy-start(bf16[128,128]{1,0:T(8,128)(2,1)} %upward.1.packed_ref) | copy-start | bytes 98308
  13.4 18.9 %all-to-all-start = ((bf16[32,32,128]{2,1,0:T(8,128)(2,1)}), bf16[32,32,128]{2,1,0:T(8,128)(2,1)S(1)}, u32[]{:S(2)}, u32[]{:S(2)}) async-start(bf16[32,32,128]{2,1,0:T(8,128)(2,1)} %get-tuple-element.18), calls=%async_computation | async-start | bytes 524288 | tf_op jit(solution)/shard_map/all_to_all | solution.py:376
  32.0 13.9 %copy-start.4 = (bf16[128,488]{0,1:T(8,128)(2,1)S(1)}, bf16[128,488]{0,1:T(8,128)(2,1)}, u32[]{:S(2)}) copy-start(bf16[128,488]{0,1:T(8,128)(2,1)} %param.13) | copy-start | bytes 374788
  32.3 13.6 %copy-start = (bf16[488,8,488]{2,1,0:T(8,128)(2,1)S(1)}, bf16[488,8,488]{2,1,0:T(8,128)(2,1)}, u32[]{:S(2)}) copy-start(bf16[488,8,488]{2,1,0:T(8,128)(2,1)} %l2l_ref.1) | copy-start | bytes 11430916
  41.7 5.6 %copy-start.1 = (bf16[1024,488]{0,1:T(8,128)(2,1)S(1)}, bf16[1024,488]{0,1:T(8,128)(2,1)}, u32[]{:S(2)}) copy-start(bf16[1024,488]{0,1:T(8,128)(2,1)} %param.15) | copy-start | bytes 2998276
  41.7 5.6 %collective-permute-start.3 = (bf16[128,128]{1,0:T(8,128)(2,1)S(1)}, bf16[128,128]{1,0:T(8,128)(2,1)S(1)}, u32[]{:S(2)}, u32[]{:S(2)}) collective-permute-start(bf16[128,128]{1,0:T(8,128)(2,1)S(1)} %get-tuple-element.20), channel_id=1, source_target_pairs={{0,2},{1,3},{2,0},{3,1},{4,6},{5,7},{6,4},{7,5},{8,10},{9,11},{10,... | collective-permute-start | bytes 98312 | tf_op jit(solution)/shard_map/ppermute | solution.py:369
  43.2 4.1 %collective-permute-start.4 = (bf16[128,128]{1,0:T(8,128)(2,1)S(1)}, bf16[128,128]{1,0:T(8,128)(2,1)S(1)}, u32[]{:S(2)}, u32[]{:S(2)}) collective-permute-start(bf16[128,128]{1,0:T(8,128)(2,1)S(1)} %get-tuple-element.21), channel_id=1, source_target_pairs={{0,1},{1,2},{2,3},{3,0},{4,5},{5,6},{6,7},{7,4},{8,9},{9,10},{10,1... | collective-permute-start | bytes 98312 | tf_op jit(solution)/shard_map/ppermute | solution.py:369
  43.2 4.1 %collective-permute-start.5 = (bf16[128,128]{1,0:T(8,128)(2,1)S(1)}, bf16[128,128]{1,0:T(8,128)(2,1)S(1)}, u32[]{:S(2)}, u32[]{:S(2)}) collective-permute-start(bf16[128,128]{1,0:T(8,128)(2,1)S(1)} %get-tuple-element.22), channel_id=1, source_target_pairs={{0,3},{1,0},{2,1},{3,2},{4,7},{5,4},{6,5},{7,6},{8,11},{9,8},{10,9... | collective-permute-start | bytes 98312 | tf_op jit(solution)/shard_map/ppermute | solution.py:369

commit v6 on v4

--- a/solution.py
+++ b/solution.py
@@ -106,12 +106,20 @@
     )
 
 
+def neighbours(part, npart):
+    return jnp.maximum(part - 1, 0), jnp.minimum(part + 1, npart - 1)
+
+
 def prep_kernel(list_ref, rows_ref, packed_ref, code_ref, hot_ref, own_ref):
     own_ref[...] = packed_ref[...]
     part = lax.axis_index("dom")
     offsets, count = list_ref.shape
-    wanted = rows_ref.shape[0]
-    hot_ref[...] = one_hot(jnp.broadcast_to(rows_ref[...], (wanted, 128)).astype(I16), count)
+    npart = rows_ref.shape[0] // CAP
+    rows = [rows_ref[p * CAP:p * CAP + SURE, :] for p in range(npart)]
+    for side in neighbours(part, npart):
+        rows.append(rows_ref[pl.ds(pl.multiple_of(side * CAP + SURE, SURE), SURE), :])
+    rows = jnp.concatenate(rows, axis=0)
+    hot_ref[...] = one_hot(jnp.broadcast_to(rows, (rows.shape[0], 128)).astype(I16), count)
     value = list_ref[...]
     source = lax.shift_right_arithmetic(value - count, 5)
     slot = value & (CAP - 1)
@@ -133,7 +141,7 @@
         "prepare",
         (
             jax.ShapeDtypeStruct((count, 128), I16),
-            jax.ShapeDtypeStruct((rows.shape[0], count), BF),
+            jax.ShapeDtypeStruct(((rows.shape[0] // CAP + 2) * SURE, count), BF),
             jax.ShapeDtypeStruct(packed.shape, BF),
         ),
         [VMEM] * 3,
@@ -150,7 +158,12 @@
     for shift, ref in enumerate((own_ref, one_ref, two_ref, three_ref)):
         start = lax.rem(me + (4 - shift), 4) * count
         part_ref[pl.ds(pl.multiple_of(start, count), count), :] = ref[...]
-    send_ref[...] = dot(hot_ref[...], part_ref[...]).astype(BF).reshape(send_ref.shape)
+    npart, _, rank = send_ref.shape
+    rows = dot(hot_ref[...], part_ref[...]).astype(BF).reshape(npart + 2, SURE, rank)
+    send_ref[:, :SURE, :] = rows[:npart]
+    send_ref[:, SURE:, :] = jnp.zeros((npart, CAP - SURE, rank), BF)
+    for i, side in enumerate(neighbours(lax.axis_index("dom"), npart)):
+        send_ref[pl.ds(side, 1), SURE:, :] = rows[npart + i:npart + i + 1]
 
 
 def pick(pieces, hot, npart):

time: 49.2 us -> 49.1 us (level)
  no operation moved by 1% of the time
where the time goes in v6:
time: 49.1 us; the launch traced here: 48.8 us
  Pallas kernels  26.2 us (53%)
  starting transfers between devices  18.4 us (37%)
  waiting for transfers between devices  2.8 us (6%)
  local copies, waits for them, and re-layouts  1.31 us (3%)
    all_to_all x1, starting transfers between devices, local(): got = lax.all_to_all(send, 'dom', 0, 0, tiled=True)  10.2 us
    pallas_call x1, Pallas kernels, far(): call(functools.partial(far_kernel, shifts), 'far', tuple((jax.ShapeDtypeS...  9.4 us
    pallas_call x1, Pallas kernels, near(): call(near_kernel, 'near', jax.ShapeDtypeStruct((count, rank), F32), [VMEM...  8.41 us
    ppermute x6, starting transfers between devices, shifted(): lax.ppermute(x, 'sub', [(i, (i + shift) % nsub) for i in range(nsub)])  8.21 us
    pallas_call x1, Pallas kernels, upward(): call(up_kernel, 'upward', jax.ShapeDtypeStruct((count, compress.shape[1])...  3.73 us
    ppermute x6, waiting for transfers between devices, shifted(): lax.ppermute(x, 'sub', [(i, (i + shift) % nsub) for i in range(nsub)])  2.52 us
    pallas_call x1, Pallas kernels, downward(): call(down_kernel, 'downward', jax.ShapeDtypeStruct(inherited_t.shape, BF)...  1.95 us
    pallas_call x1, Pallas kernels, fold(): call(fold_kernel, 'fold', jax.ShapeDtypeStruct((nkids, rank, width), BF),...  1.4 us
  transfers between devices with their start and end apart: 7, of which 4 were waited for; matrix products, arithmetic and copies ran while one was open for 1% of the time, Pallas kernels for 21%

profile of v6, /device:TPU:1, one launch (start us, length us, event | category | flops | bytes accessed | tf_op | source)
XLA Modules:
  0.0 48.8 jit_solution(8294391375779185486)
XLA Ops:
  0.0 0.0 copy-start.6
  0.0 0.0 copy-start.2
  0.0 0.0 copy-start.5
  0.0 3.7 %upward.1.packed_ref = bf16[128,128]{1,0:T(8,128)(2,1)} custom-call(bf16[488,1024]{1,0:T(8,128)(2,1)} %bitcast.8, bf16[8,488,488]{2,1,0:T(8,128)(2,1)} %m2m_ref.1, bf16[488,128]{1,0:T(8,128)(2,1)} %compress_ref.1), custom_call_target="tpu_custom_call" | custom-call | flops 487718912 | bytes 4809728 | tf_op jit(solution)/shard_map/upward/pallas_call | solution.py:80
  3.7 3.6 %collective-permute-start.2 = (bf16[128,128]{1,0:T(8,128)(2,1)}, bf16[128,128]{1,0:T(8,128)(2,1)S(1)}, u32[]{:S(2)}, u32[]{:S(2)}) collective-permute-start(bf16[128,128]{1,0:T(8,128)(2,1)} %upward.1.packed_ref), channel_id=1, source_target_pairs={{0,3},{1,0},{2,1},{3,2},{4,7},{5,4},{6,5},{7,6},{8,11},{9,8},{10,9... | collective-permute-start | bytes 98312 | tf_op jit(solution)/shard_map/ppermute | solution.py:382
  7.4 0.4 collective-permute-start.1
  7.7 0.7 %collective-permute-start = (bf16[128,128]{1,0:T(8,128)(2,1)}, bf16[128,128]{1,0:T(8,128)(2,1)S(1)}, u32[]{:S(2)}, u32[]{:S(2)}) collective-permute-start(bf16[128,128]{1,0:T(8,128)(2,1)} %upward.1.packed_ref), channel_id=1, source_target_pairs={{0,1},{1,2},{2,3},{3,0},{4,5},{5,6},{6,7},{7,4},{8,9},{9,10},{10,1... | collective-permute-start | bytes 98312 | tf_op jit(solution)/shard_map/ppermute | solution.py:382
  8.4 0.0 copy-done.6
  8.4 0.5 %reshape.4.rows_ref = s32[1024,1]{1,0:T(8,128)S(1)} reshape(s32[1,32,32]{2,1,0:T(8,128)S(1)} %copy-done.6) | data formatting | bytes 8192 | tf_op jit(solution)/shard_map/reshape | solution.py:386
  9.0 0.0 copy-done.2
  9.0 0.0 copy-start.3
  9.0 0.7 %copy-done.3 = bf16[128,128]{1,0:T(8,128)(2,1)S(1)} copy-done((bf16[128,128]{1,0:T(8,128)(2,1)S(1)}, bf16[128,128]{1,0:T(8,128)(2,1)}, u32[]{:S(2)}) %copy-start.3) | copy-done | bytes 32792
  9.7 0.3 prepare.1
  10.0 0.0 collective-permute-done.2.three_ref
  10.0 1.9 %collective-permute-done.1.two_ref = bf16[128,128]{1,0:T(8,128)(2,1)S(1)} collective-permute-done((bf16[128,128]{1,0:T(8,128)(2,1)}, bf16[128,128]{1,0:T(8,128)(2,1)S(1)}, u32[]{:S(2)}, u32[]{:S(2)}) %collective-permute-start.1) | collective-permute-done | bytes 32800 | tf_op jit(solution)/shard_map/ppermute | solution.py:382
  11.9 0.3 collective-permute-done.one_ref
  12.2 1.0 %pick.1 = (bf16[512,128]{1,0:T(8,128)(2,1)S(1)}, bf16[32,32,128]{2,1,0:T(8,128)(2,1)}) custom-call(bf16[128,128]{1,0:T(8,128)(2,1)S(1)} %get-tuple-element.15.own_ref, bf16[128,128]{1,0:T(8,128)(2,1)S(1)} %collective-permute-done.one_ref, bf16[128,128]{1,0:T(8,128)(2,1)S(1)} %collective-permute-done.1.two_ref, ...), custom_call_target="tpu_custom_call" | custom-call | flops 71303168 | bytes 557056 | tf_op jit(solution)/shard_map/pick/pallas_call | solution.py:171
  13.3 10.2 %all-to-all-start = ((bf16[32,32,128]{2,1,0:T(8,128)(2,1)}), bf16[32,32,128]{2,1,0:T(8,128)(2,1)S(1)}, u32[]{:S(2)}, u32[]{:S(2)}) async-start(bf16[32,32,128]{2,1,0:T(8,128)(2,1)} %get-tuple-element.18), calls=%async_computation | async-start | bytes 524288 | tf_op jit(solution)/shard_map/all_to_all | solution.py:389
  23.5 0.0 copy-done.5
  23.5 8.4 %near.1.near_ref = f32[512,128]{1,0:T(8,128)S(1)} custom-call(s16[512,128]{1,0:T(8,128)(2,1)S(1)} %get-tuple-element.14.code_ref, bf16[512,128]{1,0:T(8,128)(2,1)S(1)} %get-tuple-element.17.part_ref, bf16[79,128,128]{2,1,0:T(8,128)(2,1)S(1)} %copy-done.5), custom_call_target="tpu_custom_call" | custom-call | flops 6627000320 | bytes 2588672 | tf_op jit(solution)/shard_map/near/pallas_call | solution.py:265
  31.9 0.0 copy-start.4
  31.9 0.3 all-to-all-done.got_ref
  32.2 0.0 copy-start
  32.2 9.4 %far.1 = (f32[128,128]{1,0:T(8,128)S(1)}, bf16[128,128]{1,0:T(8,128)(2,1)S(1)}, bf16[128,128]{1,0:T(8,128)(2,1)S(1)}, bf16[128,128]{1,0:T(8,128)(2,1)S(1)}) custom-call(s16[512,128]{1,0:T(8,128)(2,1)S(1)} %get-tuple-element.14.code_ref, f32[512,128]{1,0:T(8,128)S(1)} %near.1.near_ref, bf16[32,32,128]{2,1,0:T(8,128)(2,1)S(1)} %all-to-all-done.got_ref, ...), custom_call_target="tpu_custom_call" | custom-call | flops 6627000320 | bytes 2588672 | tf_op jit(solution)/shard_map/far/pallas_call | solution.py:319
  41.6 0.0 copy-start.1
  41.6 0.1 collective-permute-start.3
  41.7 1.5 %collective-permute-start.4 = (bf16[128,128]{1,0:T(8,128)(2,1)S(1)}, bf16[128,128]{1,0:T(8,128)(2,1)S(1)}, u32[]{:S(2)}, u32[]{:S(2)}) collective-permute-start(bf16[128,128]{1,0:T(8,128)(2,1)S(1)} %get-tuple-element.21), channel_id=1, source_target_pairs={{0,2},{1,3},{2,0},{3,1},{4,6},{5,7},{6,4},{7,5},{8,10},{9,11},{10,... | collective-permute-start | bytes 98312 | tf_op jit(solution)/shard_map/ppermute | solution.py:382
  43.2 2.0 %collective-permute-start.5 = (bf16[128,128]{1,0:T(8,128)(2,1)S(1)}, bf16[128,128]{1,0:T(8,128)(2,1)S(1)}, u32[]{:S(2)}, u32[]{:S(2)}) collective-permute-start(bf16[128,128]{1,0:T(8,128)(2,1)S(1)} %get-tuple-element.22), channel_id=1, source_target_pairs={{0,3},{1,0},{2,1},{3,2},{4,7},{5,4},{6,5},{7,6},{8,11},{9,8},{10,9... | collective-permute-start | bytes 98312 | tf_op jit(solution)/shard_map/ppermute | solution.py:382
  45.1 0.0 copy-done.4
  45.1 0.0 copy-done
  45.2 1.4 %fold.1.fold_ref = bf16[8,128,488]{2,1,0:T(8,128)(2,1)S(1)} custom-call(bf16[488,128]{1,0:T(8,128)(2,1)S(1)} %bitcast.7, bf16[488,8,488]{2,1,0:T(8,128)(2,1)S(1)} %copy-done), custom_call_target="tpu_custom_call" | custom-call | flops 487718912 | bytes 3810304 | tf_op jit(solution)/shard_map/fold/pallas_call | solution.py:201
  46.6 0.0 collective-permute-done.3.one_ref
  46.6 0.0 collective-permute-done.4.two_ref
  46.6 0.3 collective-permute-done.5.three_ref
  46.9 0.0 copy-done.1
  46.9 2.0 %downward.1 = bf16[488,1024]{1,0:T(8,128)(2,1)} custom-call(f32[128,128]{1,0:T(8,128)S(1)} %get-tuple-element.19.own_ref, bf16[128,128]{1,0:T(8,128)(2,1)S(1)} %collective-permute-done.3.one_ref, bf16[128,128]{1,0:T(8,128)(2,1)S(1)} %collective-permute-done.4.two_ref, bf16[128,128]{1,0:T(8,128)(2,1)S(1)} %collective-permute-done.5.three_ref, ...), custom_call_target="tpu_custom_call" | custom-call | flops 127926272 | bytes 2998272 | tf_op jit(solution)/shard_map/downward/pallas_call | solution.py:366
Async XLA Ops:
  0.0 8.4 %copy-start.6 = (s32[1,32,32]{2,1,0:T(8,128)S(1)}, s32[1,32,32]{2,1,0:T(8,128)}, u32[]{:S(2)}) copy-start(s32[1,32,32]{2,1,0:T(8,128)} %param.16) | copy-start | bytes 12292
  0.0 9.0 %copy-start.2 = (s32[512,79]{0,1:T(8,128)S(1)}, s32[512,79]{0,1:T(8,128)}, u32[]{:S(2)}) copy-start(s32[512,79]{0,1:T(8,128)} %param.17) | copy-start | bytes 485380
  0.0 23.5 %copy-start.5 = (bf16[79,128,128]{2,1,0:T(8,128)(2,1)S(1)}, bf16[79,128,128]{2,1,0:T(8,128)(2,1)}, u32[]{:S(2)}) copy-start(bf16[79,128,128]{2,1,0:T(8,128)(2,1)} %core_ref.3) | copy-start | bytes 7766020
  3.7 6.2 %collective-permute-start.2 = (bf16[128,128]{1,0:T(8,128)(2,1)}, bf16[128,128]{1,0:T(8,128)(2,1)S(1)}, u32[]{:S(2)}, u32[]{:S(2)}) collective-permute-start(bf16[128,128]{1,0:T(8,128)(2,1)} %upward.1.packed_ref), channel_id=1, source_target_pairs={{0,3},{1,0},{2,1},{3,2},{4,7},{5,4},{6,5},{7,6},{8,11},{9,8},{10,9... | collective-permute-start | bytes 98312 | tf_op jit(solution)/shard_map/ppermute | solution.py:382
  7.4 4.5 %collective-permute-start.1 = (bf16[128,128]{1,0:T(8,128)(2,1)}, bf16[128,128]{1,0:T(8,128)(2,1)S(1)}, u32[]{:S(2)}, u32[]{:S(2)}) collective-permute-start(bf16[128,128]{1,0:T(8,128)(2,1)} %upward.1.packed_ref), channel_id=1, source_target_pairs={{0,2},{1,3},{2,0},{3,1},{4,6},{5,7},{6,4},{7,5},{8,10},{9,11},{10,... | collective-permute-start | bytes 98312 | tf_op jit(solution)/shard_map/ppermute | solution.py:382
  7.7 4.5 %collective-permute-start = (bf16[128,128]{1,0:T(8,128)(2,1)}, bf16[128,128]{1,0:T(8,128)(2,1)S(1)}, u32[]{:S(2)}, u32[]{:S(2)}) collective-permute-start(bf16[128,128]{1,0:T(8,128)(2,1)} %upward.1.packed_ref), channel_id=1, source_target_pairs={{0,1},{1,2},{2,3},{3,0},{4,5},{5,6},{6,7},{7,4},{8,9},{9,10},{10,1... | collective-permute-start | bytes 98312 | tf_op jit(solution)/shard_map/ppermute | solution.py:382
  9.0 0.8 %copy-start.3 = (bf16[128,128]{1,0:T(8,128)(2,1)S(1)}, bf16[128,128]{1,0:T(8,128)(2,1)}, u32[]{:S(2)}) copy-start(bf16[128,128]{1,0:T(8,128)(2,1)} %upward.1.packed_ref) | copy-start | bytes 98308
  13.3 18.9 %all-to-all-start = ((bf16[32,32,128]{2,1,0:T(8,128)(2,1)}), bf16[32,32,128]{2,1,0:T(8,128)(2,1)S(1)}, u32[]{:S(2)}, u32[]{:S(2)}) async-start(bf16[32,32,128]{2,1,0:T(8,128)(2,1)} %get-tuple-element.18), calls=%async_computation | async-start | bytes 524288 | tf_op jit(solution)/shard_map/all_to_all | solution.py:389
  31.9 13.2 %copy-start.4 = (bf16[128,488]{0,1:T(8,128)(2,1)S(1)}, bf16[128,488]{0,1:T(8,128)(2,1)}, u32[]{:S(2)}) copy-start(bf16[128,488]{0,1:T(8,128)(2,1)} %param.13) | copy-start | bytes 374788
  32.2 13.0 %copy-start = (bf16[488,8,488]{2,1,0:T(8,128)(2,1)S(1)}, bf16[488,8,488]{2,1,0:T(8,128)(2,1)}, u32[]{:S(2)}) copy-start(bf16[488,8,488]{2,1,0:T(8,128)(2,1)} %l2l_ref.1) | copy-start | bytes 11430916
  41.6 5.3 %copy-start.1 = (bf16[1024,488]{0,1:T(8,128)(2,1)S(1)}, bf16[1024,488]{0,1:T(8,128)(2,1)}, u32[]{:S(2)}) copy-start(bf16[1024,488]{0,1:T(8,128)(2,1)} %param.15) | copy-start | bytes 2998276
  41.6 5.0 %collective-permute-start.3 = (bf16[128,128]{1,0:T(8,128)(2,1)S(1)}, bf16[128,128]{1,0:T(8,128)(2,1)S(1)}, u32[]{:S(2)}, u32[]{:S(2)}) collective-permute-start(bf16[128,128]{1,0:T(8,128)(2,1)S(1)} %get-tuple-element.20), channel_id=1, source_target_pairs={{0,1},{1,2},{2,3},{3,0},{4,5},{5,6},{6,7},{7,4},{8,9},{9,10},{10,1... | collective-permute-start | bytes 98312 | tf_op jit(solution)/shard_map/ppermute | solution.py:382
  41.7 4.9 %collective-permute-start.4 = (bf16[128,128]{1,0:T(8,128)(2,1)S(1)}, bf16[128,128]{1,0:T(8,128)(2,1)S(1)}, u32[]{:S(2)}, u32[]{:S(2)}) collective-permute-start(bf16[128,128]{1,0:T(8,128)(2,1)S(1)} %get-tuple-element.21), channel_id=1, source_target_pairs={{0,2},{1,3},{2,0},{3,1},{4,6},{5,7},{6,4},{7,5},{8,10},{9,11},{10,... | collective-permute-start | bytes 98312 | tf_op jit(solution)/shard_map/ppermute | solution.py:382
  43.2 3.7 %collective-permute-start.5 = (bf16[128,128]{1,0:T(8,128)(2,1)S(1)}, bf16[128,128]{1,0:T(8,128)(2,1)S(1)}, u32[]{:S(2)}, u32[]{:S(2)}) collective-permute-start(bf16[128,128]{1,0:T(8,128)(2,1)S(1)} %get-tuple-element.22), channel_id=1, source_target_pairs={{0,3},{1,0},{2,1},{3,2},{4,7},{5,4},{6,5},{7,6},{8,11},{9,8},{10,9... | collective-permute-start | bytes 98312 | tf_op jit(solution)/shard_map/ppermute | solution.py:382
